TPU v7x, 128 devices: a whole 4x4x4 slice. The times are simulated.
128 devices in a mesh: tm: 8 (over y, core), space: 16 (over x, z).
Axes of the slice: x: 4, y: 4, z: 4, core: 2. Of those that a mesh axis runs over, the one named last changes fastest.
Arguments:
- queries: bfloat16 [16384, 6144], P(('tm', 'space')), may hold values from -5 to 5
- key_rows: bfloat16 [16384, 6144], P(('tm', 'space')), may hold values from -5 to 5
- value_rows: bfloat16 [16384, 6144], P(('tm', 'space')), may hold values from -6 to 6
- tile_lists: int32 [8, 32, 2], P('tm'), may hold values from 0 to 31, as said below
- span_reach: int32 [8, 32], P('tm'), may hold values from 0 to 7, as said below
Outputs:
- attended: bfloat16 [16384, 6144], P(('tm', 'space'))
Inputs may be any that keep to these rules, and one draw needn't show every extreme that they name: Each row of tile_lists holds 2 different tiles and begins with the query tile itself. span_reach[c, t] <= c for every span c and tile t; in the last span, tile 0 reaches span 0 and tile 1 reaches only its own span.
All inputs are finite; a program needn't handle non-finite values.
Results may differ from a plain program's by a relative error of at most 0.009.
Values may be sent and summed in bfloat16 or wider, within the bound.
A program may use at most 192 MiB of HBM per device.

v0:
```python
import jax
import jax.numpy as jnp
from jax import lax
from jax.sharding import PartitionSpec as P

DH = 128
TILE = 64
KT = 2


def merge_state(carry, state):
    numer_a, top_a, total_a = carry
    numer_b, top_b, total_b = state
    big = jnp.maximum(top_a, top_b)
    factor_a = jnp.exp(top_a - big)
    factor_b = jnp.exp(top_b - big)
    numer = factor_a[..., None] * numer_a + factor_b[..., None] * numer_b
    return (numer, big, factor_a * total_a + factor_b * total_b)


def body(queries, key_rows, value_rows, tile_lists, span_reach):
    groups = lax.axis_size("space")
    tok_rows = queries.shape[0]
    heads_local = queries.shape[1] // DH // groups
    lists = tile_lists[0]
    reach = span_reach[0][:, None, None]
    span = lax.axis_index("tm")
    scale = DH ** (-0.5)
    shape_split = (tok_rows, groups, heads_local, DH)
    query_part = lax.all_to_all(
        queries.reshape(shape_split), "space", split_axis=1, concat_axis=0, tiled=True
    )
    key_part = lax.all_to_all(
        key_rows.reshape(shape_split), "space", split_axis=1, concat_axis=0, tiled=True
    )
    value_part = lax.all_to_all(
        value_rows.reshape(shape_split), "space", split_axis=1, concat_axis=0, tiled=True
    )
    span_rows = query_part.shape[0]
    heads_here = query_part.shape[2]
    tiles = span_rows // TILE
    query_tiles = query_part.reshape(tiles, TILE, heads_here, DH)
    flat_width = heads_here * DH
    stacked = jnp.stack(
        [key_part.reshape(span_rows, flat_width), value_part.reshape(span_rows, flat_width)]
    )
    initial = (
        jnp.zeros((tiles, heads_here, TILE, DH), jnp.float32),
        jnp.full((tiles, heads_here, TILE), -1e30, jnp.float32),
        jnp.zeros((tiles, heads_here, TILE), jnp.float32),
    )
    carry = initial
    pieces = lax.all_gather(stacked[None], "tm", axis=0, tiled=True)
    start = jnp.int32(0)
    for offset in range(pieces.shape[0]):
        piece_stacked = pieces[offset]
        source = start + offset
        key_sel = (
            piece_stacked[0]
            .reshape(tiles, TILE, heads_here, DH)[lists]
            .reshape(tiles, KT * TILE, heads_here, DH)
        )
        value_sel = (
            piece_stacked[1]
            .reshape(tiles, TILE, heads_here, DH)[lists]
            .reshape(tiles, KT * TILE, heads_here, DH)
        )
        scores = (
            jnp.einsum("tqhd,tkhd->thqk", query_tiles, key_sel, preferred_element_type=jnp.float32)
            * scale
        )
        top = jnp.max(scores, axis=-1)
        expo = jnp.exp(scores - top[..., None])
        total = jnp.sum(expo, axis=-1)
        weights = expo.astype(jnp.bfloat16)
        partial_value = jnp.einsum(
            "thqk,tkhd->thqd", weights, value_sel, preferred_element_type=jnp.float32
        )
        valid = jnp.logical_and(source >= reach, source <= span)
        top = jnp.where(valid, top, jnp.float32(-1e30))
        total = jnp.where(valid, total, jnp.float32(0.0))
        partial_value = jnp.where(valid[..., None], partial_value, jnp.float32(0.0))
        carry = merge_state(carry, (partial_value, top, total))
    numer, big, denom = carry
    output = numer / denom[..., None]
    regrouped = (
        jnp.transpose(output, (0, 2, 1, 3)).reshape(span_rows, heads_here, DH).astype(jnp.bfloat16)
    )
    flat_out = regrouped.reshape(regrouped.shape[0], heads_local * DH)
    return lax.all_to_all(flat_out, "space", split_axis=0, concat_axis=1, tiled=True)


def solution(mesh):
    in_specs = (
        P(("tm", "space"), None),
        P(("tm", "space"), None),
        P(("tm", "space"), None),
        P("tm", None, None),
        P("tm", None),
    )
    out_specs = P(("tm", "space"), None)
    return jax.shard_map(body, mesh=mesh, in_specs=in_specs, out_specs=out_specs, check_vma=False)
```

profile of v0, /device:TPU:24, one launch (start us, length us, event | category | flops | bytes accessed | tf_op | source)
XLA Modules:
  0.0 575.3 jit_solution(2841472028991013847)
XLA Ops:
  9.3 7.9 %all-to-all-start = ((bf16[128,16,3,128]{0,3,2,1:T(8,128)(2,1)}), bf16[128,16,3,128]{0,3,2,1:T(8,128)(2,1)S(1)}, u32[]{:S(2)}, u32[]{:S(2)}) async-start(bf16[128,16,3,128]{0,3,2,1:T(8,128)(2,1)} %bitcast.1), calls=%async_computation | async-start | bytes 3145728 | tf_op jit(solution)/shard_map/all_to_all | solution.py:33
  18.7 22.2 %all-to-all-done = bf16[128,16,3,128]{0,3,2,1:T(8,128)(2,1)S(1)} async-done(((bf16[128,16,3,128]{0,3,2,1:T(8,128)(2,1)}), bf16[128,16,3,128]{0,3,2,1:T(8,128)(2,1)S(1)}, u32[]{:S(2)}, u32[]{:S(2)}) %all-to-all-start) | async-done | bytes 1572896 | tf_op jit(solution)/shard_map/all_to_all | solution.py:33
  50.7 15.8 %all-to-all-done.1 = bf16[128,16,3,128]{0,3,2,1:T(8,128)(2,1)S(1)} async-done(((bf16[128,16,3,128]{0,3,2,1:T(8,128)(2,1)}), bf16[128,16,3,128]{0,3,2,1:T(8,128)(2,1)S(1)}, u32[]{:S(2)}, u32[]{:S(2)}) %all-to-all-start.1) | async-done | bytes 1572896 | tf_op jit(solution)/shard_map/all_to_all | solution.py:36
  82.6 19.5 %all-to-all-done.2 = bf16[128,16,3,128]{0,3,2,1:T(8,128)(2,1)S(1)} async-done(((bf16[128,16,3,128]{0,3,2,1:T(8,128)(2,1)}), bf16[128,16,3,128]{0,3,2,1:T(8,128)(2,1)S(1)}, u32[]{:S(2)}, u32[]{:S(2)}) %all-to-all-start.2) | async-done | bytes 1572896 | tf_op jit(solution)/shard_map/all_to_all | solution.py:30
  103.0 89.0 %all-gather.3.cloned.1.call-done = bf16[16,2048,384]{2,1,0:T(8,128)(2,1)} async-done(((bf16[2,2048,384]{2,1,0:T(8,128)(2,1)}), bf16[16,2048,384]{2,1,0:T(8,128)(2,1)}) %all-gather.3.cloned.1.call-update) | async-done | bytes 25165840 | tf_op jit(solution)/shard_map/all_gather | solution.py:53
  192.0 16.9 %fusion.151 = (bf16[1,1,2048,384]{3,2,1,0:T(8,128)(2,1)}, bf16[1,1,2048,384]{3,2,1,0:T(8,128)(2,1)}, bf16[1,1,2048,384]{3,2,1,0:T(8,128)(2,1)}, bf16[1,1,2048,38...) fusion(bf16[8,2,2048,384]{3,2,1,0:T(8,128)(2,1)} %bitcast.400), kind=kLoop, calls=%fused_computation.213 | loop fusion | bytes 50331648 | tf_op jit(solution)/shard_map/slice | solution.py:59
  216.2 7.9 %gather_fusion.5 = bf16[64,64,3,128]{3,2,1,0:T(4,128)(2,1)} fusion(bf16[32,64,3,128]{3,2,1,0:T(4,128)(2,1)} %reshape_squeeze.53, s32[1024]{0:T(1024)S(1)} %pad_clamp_fusion), kind=kCustom, calls=%fused_computation.5 | custom fusion | bytes 6291712 | tf_op jit(solution)/shard_map/gather | solution.py:59
  224.1 8.0 %gather_fusion.4 = bf16[64,64,3,128]{3,2,1,0:T(4,128)(2,1)} fusion(bf16[32,64,3,128]{3,2,1,0:T(4,128)(2,1)} %reshape_squeeze.52, s32[1024]{0:T(1024)S(1)} %pad_clamp_fusion), kind=kCustom, calls=%fused_computation.4 | custom fusion | bytes 6291712 | tf_op jit(solution)/shard_map/gather | solution.py:59
  283.0 6.7 %gather_fusion.1 = bf16[64,64,3,128]{3,2,1,0:T(4,128)(2,1)} fusion(bf16[32,64,3,128]{3,2,1,0:T(4,128)(2,1)S(1)} %reshape_squeeze.49, s32[1024]{0:T(1024)S(1)} %pad_clamp_fusion), kind=kCustom, calls=%fused_computation.1 | custom fusion | bytes 6291712 | tf_op jit(solution)/shard_map/gather | solution.py:59
  300.0 7.9 %gather_fusion = bf16[64,64,3,128]{3,2,1,0:T(4,128)(2,1)} fusion(bf16[32,64,3,128]{3,2,1,0:T(4,128)(2,1)} %reshape_squeeze.48, s32[1024]{0:T(1024)S(1)} %pad_clamp_fusion), kind=kCustom, calls=%fused_computation | custom fusion | bytes 6291712 | tf_op jit(solution)/shard_map/gather | solution.py:59
  307.9 7.2 %bitcast_reduce_fusion.7 = (f32[32,3,64]{2,1,0:T(4,128)}, f32[32,3,128,64]{2,3,1,0:T(8,128)}) fusion(bf16[32,64,3,128]{3,1,0,2:T(8,128)(2,1)} %bitcast.397, bf16[32,128,3,128]{3,2,1,0:T(4,128)(2,1)} %bitcast.414), kind=kOutput, calls=%fused_computation.94 | convolution fusion | flops 202893312 | bytes 7888896 | tf_op jit(solution)/shard_map/tqhd,tkhd->thqk/dot_general | solution.py:69
  320.3 7.9 %gather_fusion.7 = bf16[64,64,3,128]{3,2,1,0:T(4,128)(2,1)} fusion(bf16[32,64,3,128]{3,2,1,0:T(4,128)(2,1)} %reshape_squeeze.55, s32[1024]{0:T(1024)S(1)} %pad_clamp_fusion), kind=kCustom, calls=%fused_computation.7 | custom fusion | bytes 6291712 | tf_op jit(solution)/shard_map/gather | solution.py:59
  340.1 8.1 %gather_fusion.6 = bf16[64,64,3,128]{3,2,1,0:T(4,128)(2,1)} fusion(bf16[32,64,3,128]{3,2,1,0:T(4,128)(2,1)} %reshape_squeeze.54, s32[1024]{0:T(1024)S(1)} %pad_clamp_fusion), kind=kCustom, calls=%fused_computation.6 | custom fusion | bytes 6291712 | tf_op jit(solution)/shard_map/gather | solution.py:59
  348.2 7.2 %bitcast_reduce_fusion.1 = (f32[32,3,64]{2,1,0:T(4,128)}, f32[32,3,128,64]{2,3,1,0:T(8,128)}) fusion(bf16[32,64,3,128]{3,1,0,2:T(8,128)(2,1)} %bitcast.399, bf16[32,128,3,128]{3,2,1,0:T(4,128)(2,1)} %bitcast.410), kind=kOutput, calls=%fused_computation.64 | convolution fusion | flops 202893312 | bytes 7888896 | tf_op jit(solution)/shard_map/tqhd,tkhd->thqk/dot_general | solution.py:69
  360.6 8.0 %gather_fusion.10 = bf16[64,64,3,128]{3,2,1,0:T(4,128)(2,1)} fusion(bf16[32,64,3,128]{3,2,1,0:T(4,128)(2,1)} %reshape_squeeze.58, s32[1024]{0:T(1024)S(1)} %pad_clamp_fusion), kind=kCustom, calls=%fused_computation.10 | custom fusion | bytes 6291712 | tf_op jit(solution)/shard_map/gather | solution.py:64
  373.7 7.9 %gather_fusion.9 = bf16[64,64,3,128]{3,2,1,0:T(4,128)(2,1)} fusion(bf16[32,64,3,128]{3,2,1,0:T(4,128)(2,1)} %reshape_squeeze.57, s32[1024]{0:T(1024)S(1)} %pad_clamp_fusion), kind=kCustom, calls=%fused_computation.9 | custom fusion | bytes 6291712 | tf_op jit(solution)/shard_map/gather | solution.py:64
  386.9 8.1 %gather_fusion.11 = bf16[64,64,3,128]{3,2,1,0:T(4,128)(2,1)} fusion(bf16[32,64,3,128]{3,2,1,0:T(4,128)(2,1)} %reshape_squeeze.59, s32[1024]{0:T(1024)S(1)} %pad_clamp_fusion), kind=kCustom, calls=%fused_computation.11 | custom fusion | bytes 6291712 | tf_op jit(solution)/shard_map/gather | solution.py:64
  413.7 8.0 %gather_fusion.12 = bf16[64,64,3,128]{3,2,1,0:T(4,128)(2,1)} fusion(bf16[32,64,3,128]{3,2,1,0:T(4,128)(2,1)} %reshape_squeeze.60, s32[1024]{0:T(1024)S(1)} %pad_clamp_fusion), kind=kCustom, calls=%fused_computation.12 | custom fusion | bytes 6291712 | tf_op jit(solution)/shard_map/gather | solution.py:64
  426.8 8.0 %gather_fusion.13 = bf16[64,64,3,128]{3,2,1,0:T(4,128)(2,1)} fusion(bf16[32,64,3,128]{3,2,1,0:T(4,128)(2,1)} %reshape_squeeze.61, s32[1024]{0:T(1024)S(1)} %pad_clamp_fusion), kind=kCustom, calls=%fused_computation.13 | custom fusion | bytes 6291712 | tf_op jit(solution)/shard_map/gather | solution.py:64
  453.4 8.4 %gather_fusion.14 = bf16[64,64,3,128]{3,2,1,0:T(4,128)(2,1)} fusion(bf16[32,64,3,128]{3,2,1,0:T(4,128)(2,1)} %reshape_squeeze.62, s32[1024]{0:T(1024)S(1)} %pad_clamp_fusion), kind=kCustom, calls=%fused_computation.14 | custom fusion | bytes 6291712 | tf_op jit(solution)/shard_map/gather | solution.py:64
  466.9 8.0 %gather_fusion.15 = bf16[64,64,3,128]{3,2,1,0:T(4,128)(2,1)} fusion(bf16[32,64,3,128]{3,2,1,0:T(4,128)(2,1)} %reshape_squeeze.63, s32[1024]{0:T(1024)S(1)} %pad_clamp_fusion), kind=kCustom, calls=%fused_computation.15 | custom fusion | bytes 6291712 | tf_op jit(solution)/shard_map/gather | solution.py:64
  493.5 8.0 %gather_fusion.8 = bf16[64,64,3,128]{3,2,1,0:T(4,128)(2,1)} fusion(bf16[32,64,3,128]{3,2,1,0:T(4,128)(2,1)} %reshape_squeeze.56, s32[1024]{0:T(1024)S(1)} %pad_clamp_fusion), kind=kCustom, calls=%fused_computation.8 | custom fusion | bytes 6291712 | tf_op jit(solution)/shard_map/gather | solution.py:64
  511.9 19.4 %fusion.2 = bf16[32,64,3,128]{3,1,2,0:T(8,128)(2,1)S(1)} fusion(f32[32,3,64,128]{3,2,1,0:T(8,128)} %fusion.3, f32[32,3,64,128]{3,2,1,0:T(8,128)} %fusion.7, f32[32,3,64,128]{3,2,1,0:T(8,128)} %fusion.11, f32[32,3,64,128]{3,2,1,0:T(8,128)S(1)} %copy-done.14, f32[32,3,64,128]{3,2,1,0:T(8,128)S(1)} %copy-done.13, f32[32,3,64,128]{3,2,1,0:T(8,128)S(1)} %copy-done.12, ...), kind=kOutput, calls=%fused_computation.20 | convolution fusion | flops 229638144 | bytes 30327040 | tf_op jit(solution)/shard_map/thqk,tkhd->thqd/dot_general | solution.py:76
  535.3 30.4 %all_to_all.61 = bf16[16,128,384]{2,1,0:T(8,128)(2,1)S(1)} all-to-all(bf16[16,128,384]{2,1,0:T(8,128)(2,1)} %convert_element_type.41), channel_id=1, replica_groups=mesh['tm'=8,'space'=16] {'space'}, dimensions={0} | all-to-all | bytes 3145728 | tf_op jit(solution)/shard_map/all_to_all | solution.py:90
  (126 shorter events, 214.7 us)
Async XLA Ops:
  6.5 10.6 %copy-start.15 = (bf16[128,6144]{1,0:T(8,128)(2,1)S(1)}, bf16[128,6144]{1,0:T(8,128)(2,1)}, u32[]{:S(2)}) copy-start(bf16[128,6144]{1,0:T(8,128)(2,1)} %param.7) | copy-start | bytes 4718596
  9.3 31.7 %all-to-all-start = ((bf16[128,16,3,128]{0,3,2,1:T(8,128)(2,1)}), bf16[128,16,3,128]{0,3,2,1:T(8,128)(2,1)S(1)}, u32[]{:S(2)}, u32[]{:S(2)}) async-start(bf16[128,16,3,128]{0,3,2,1:T(8,128)(2,1)} %bitcast.1), calls=%async_computation | async-start | bytes 3145728 | tf_op jit(solution)/shard_map/all_to_all | solution.py:33
  40.9 25.6 %all-to-all-start.1 = ((bf16[128,16,3,128]{0,3,2,1:T(8,128)(2,1)}), bf16[128,16,3,128]{0,3,2,1:T(8,128)(2,1)S(1)}, u32[]{:S(2)}, u32[]{:S(2)}) async-start(bf16[128,16,3,128]{0,3,2,1:T(8,128)(2,1)} %bitcast.4), calls=%async_computation.1 | async-start | bytes 3145728 | tf_op jit(solution)/shard_map/all_to_all | solution.py:36
  44.8 147.2 %all-gather.3.cloned.1.call-start = ((), (), s32[]{:S(2)}) async-start(), calls=%async_computation.4 | async-start | bytes 28311552 | tf_op jit(solution)/shard_map/all_gather | solution.py:53
  77.6 24.6 %all-to-all-start.2 = ((bf16[128,16,3,128]{0,3,2,1:T(8,128)(2,1)}), bf16[128,16,3,128]{0,3,2,1:T(8,128)(2,1)S(1)}, u32[]{:S(2)}, u32[]{:S(2)}) async-start(bf16[128,16,3,128]{0,3,2,1:T(8,128)(2,1)} %bitcast.10), calls=%async_computation.2 | async-start | bytes 3145728 | tf_op jit(solution)/shard_map/all_to_all | solution.py:30
  103.0 129.0 %copy-start = (bf16[16,128,1,3,128]{4,1,0,3,2:T(8,128)(2,1)}, bf16[16,128,1,3,128]{4,1,0,3,2:T(8,128)(2,1)S(1)}, u32[]{:S(2)}) copy-start(bf16[16,128,1,3,128]{4,1,0,3,2:T(8,128)(2,1)S(1)} %copy.145) | copy-start | bytes 4718596
  434.7 6.1 %copy-start.2 = (f32[32,3,128,64]{2,3,1,0:T(8,128)S(1)}, f32[32,3,128,64]{2,3,1,0:T(8,128)}, u32[]{:S(2)}) copy-start(f32[32,3,128,64]{2,3,1,0:T(8,128)} %get-tuple-element.59) | copy-start | bytes 9437188
  501.5 8.9 %copy-start.19 = (f32[32,3,64]{2,1,0:T(4,128)S(1)}, f32[32,3,64]{2,1,0:T(4,128)}, u32[]{:S(2)}) copy-start(f32[32,3,64]{2,1,0:T(4,128)} %get-tuple-element.66) | copy-start | bytes 73732
  501.5 8.9 %copy-start.26 = (pred[32]{0:T(512)(128)(4,1)S(1)}, pred[32]{0:T(512)(128)(4,1)}, u32[]{:S(2)}) copy-start(pred[32]{0:T(512)(128)(4,1)} %get-tuple-element.47) | copy-start | bytes 100
  501.5 8.9 %copy-start.27 = (pred[32]{0:T(512)(128)(4,1)S(1)}, pred[32]{0:T(512)(128)(4,1)}, u32[]{:S(2)}) copy-start(pred[32]{0:T(512)(128)(4,1)} %get-tuple-element.48) | copy-start | bytes 100
  501.5 8.9 %copy-start.28 = (pred[32]{0:T(512)(128)(4,1)S(1)}, pred[32]{0:T(512)(128)(4,1)}, u32[]{:S(2)}) copy-start(pred[32]{0:T(512)(128)(4,1)} %get-tuple-element.49) | copy-start | bytes 100
  501.5 9.2 %copy-start.18 = (f32[32,3,64]{2,1,0:T(4,128)S(1)}, f32[32,3,64]{2,1,0:T(4,128)}, u32[]{:S(2)}) copy-start(f32[32,3,64]{2,1,0:T(4,128)} %get-tuple-element.54) | copy-start | bytes 73732
  501.5 9.2 %copy-start.20 = (f32[32,3,64]{2,1,0:T(4,128)S(1)}, f32[32,3,64]{2,1,0:T(4,128)}, u32[]{:S(2)}) copy-start(f32[32,3,64]{2,1,0:T(4,128)} %get-tuple-element.70) | copy-start | bytes 73732
  501.5 9.2 %copy-start.21 = (f32[32,3,64]{2,1,0:T(4,128)S(1)}, f32[32,3,64]{2,1,0:T(4,128)}, u32[]{:S(2)}) copy-start(f32[32,3,64]{2,1,0:T(4,128)} %get-tuple-element.71) | copy-start | bytes 73732
  501.5 9.2 %copy-start.22 = (f32[32,3,64]{2,1,0:T(4,128)S(1)}, f32[32,3,64]{2,1,0:T(4,128)}, u32[]{:S(2)}) copy-start(f32[32,3,64]{2,1,0:T(4,128)} %get-tuple-element.72) | copy-start | bytes 73732
  501.5 9.2 %copy-start.23 = (f32[32,3,64]{2,1,0:T(4,128)S(1)}, f32[32,3,64]{2,1,0:T(4,128)}, u32[]{:S(2)}) copy-start(f32[32,3,64]{2,1,0:T(4,128)} %get-tuple-element.73) | copy-start | bytes 73732
  501.5 9.2 %copy-start.24 = (f32[32,3,64]{2,1,0:T(4,128)S(1)}, f32[32,3,64]{2,1,0:T(4,128)}, u32[]{:S(2)}) copy-start(f32[32,3,64]{2,1,0:T(4,128)} %get-tuple-element.74) | copy-start | bytes 73732
  501.6 9.2 %copy-start.25 = (f32[32,3,64]{2,1,0:T(4,128)S(1)}, f32[32,3,64]{2,1,0:T(4,128)}, u32[]{:S(2)}) copy-start(f32[32,3,64]{2,1,0:T(4,128)} %get-tuple-element.75) | copy-start | bytes 73732
  501.6 9.2 %copy-start.29 = (pred[32]{0:T(512)(128)(4,1)S(1)}, pred[32]{0:T(512)(128)(4,1)}, u32[]{:S(2)}) copy-start(pred[32]{0:T(512)(128)(4,1)} %get-tuple-element.50) | copy-start | bytes 100
  501.6 9.2 %copy-start.30 = (pred[32]{0:T(512)(128)(4,1)S(1)}, pred[32]{0:T(512)(128)(4,1)}, u32[]{:S(2)}) copy-start(pred[32]{0:T(512)(128)(4,1)} %get-tuple-element.51) | copy-start | bytes 100
  501.6 10.3 %copy-start.13 = (f32[32,3,64,128]{3,2,1,0:T(8,128)S(1)}, f32[32,3,64,128]{3,2,1,0:T(8,128)}, u32[]{:S(2)}) copy-start(f32[32,3,64,128]{3,2,1,0:T(8,128)} %fusion.19) | copy-start | bytes 9437188
  501.6 10.3 %copy-start.14 = (f32[32,3,64,128]{3,2,1,0:T(8,128)S(1)}, f32[32,3,64,128]{3,2,1,0:T(8,128)}, u32[]{:S(2)}) copy-start(f32[32,3,64,128]{3,2,1,0:T(8,128)} %fusion.15) | copy-start | bytes 9437188
  505.0 6.9 %copy-start.11 = (bf16[64,64,3,128]{3,2,1,0:T(4,128)(2,1)S(1)}, bf16[64,64,3,128]{3,2,1,0:T(4,128)(2,1)}, u32[]{:S(2)}) copy-start(bf16[64,64,3,128]{3,2,1,0:T(4,128)(2,1)} %gather_fusion.8) | copy-start | bytes 9437188
  505.0 6.9 %copy-start.12 = (f32[32,3,64,128]{3,2,1,0:T(8,128)S(1)}, f32[32,3,64,128]{3,2,1,0:T(8,128)}, u32[]{:S(2)}) copy-start(f32[32,3,64,128]{3,2,1,0:T(8,128)} %fusion.23) | copy-start | bytes 9437188
  (13 other events, 66.2 us)
Sparse Core Ops, SparseCore 0:
  74.7 117.2 all-gather.2
where the time goes:
time: 583 us; the launch traced here: 575 us
  local copies, waits for them, and re-layouts  243 us (42%)
  waiting for transfers between devices  146 us (25%)
  matrix products  102 us (17%)
  blocking collectives  30.4 us (5%)
  other arithmetic  22.8 us (4%)
  starting transfers between devices  16 us (3%)
  between operations  14.1 us (2%)
    all_gather x1, waiting for transfers between devices, body(): pieces = lax.all_gather(stacked[None], 'tm', axis=0, tiled=True)  89 us
    gather x8, local copies, waits for them, and re-layouts, body(): piece_stacked[1].reshape(tiles, TILE, heads_here, DH)[lists]  64.3 us
    gather x8, local copies, waits for them, and re-layouts, body(): piece_stacked[0].reshape(tiles, TILE, heads_here, DH)[lists]  59.6 us
    dot_general x8, matrix products, body(): jnp.einsum('tqhd,tkhd->thqk', query_tiles, key_sel, preferred_element_typ...  52.4 us
    dot_general x8, matrix products, body(): jnp.einsum('thqk,tkhd->thqd', weights, value_sel, preferred_element_type=...  50 us
    another operation x8, local copies, waits for them, and re-layouts, body(): value_sel = piece_stacked[1].reshape(tiles, TILE, heads_here, DH)[lists]....  41.1 us
    another operation x8, local copies, waits for them, and re-layouts, body(): key_sel = piece_stacked[0].reshape(tiles, TILE, heads_here, DH)[lists].re...  34.4 us
    all_to_all x1, blocking collectives, body(): lax.all_to_all(flat_out, 'space', split_axis=0, concat_axis=1, tiled=True)  30.4 us
  transfers between devices with their start and end apart: 4, of which 4 were waited for; matrix products, arithmetic and copies ran while one was open for 2% of the time, Pallas kernels for 0%

commit v1 on v0

v1 whole, which is shorter than its diff:
```python
import functools
import math

import jax
import jax.numpy as jnp
from jax import lax
from jax.experimental import pallas as pl
from jax.experimental.pallas import tpu as pltpu
from jax.sharding import PartitionSpec as P

MESH = pl.DeviceIdType.MESH
DH = 128
TILE = 64
SIDE = 4
CHIPS = 64
HEADS = 48
SPANS = 8
TILES = 32
NEG = -1e30


def offset(i):
    v = (33 * i) % CHIPS
    a, b, c = v % 4, (v // 4) % 4, v // 16
    return (3 * a) % 4, (3 * b + c) % 4, (3 * c) % 4


def kernel(
    q_in, k_in, v_in, meta_in, out, qbuf, kbuf, vbuf, obuf, meta_v, meta_s,
    q_send, k_send, v_send, o_send, m_send, q_recv, k_recv, v_recv, o_recv, m_recv,
    fk_send, fk_recv, fv_send, fv_recv, m_copy,
):
    tm = lax.axis_index("tm")
    sp = lax.axis_index("space")
    y, core = tm // 2, tm % 2
    x, z = sp // SIDE, sp % SIDE
    here = lax.rem(y + SIDE - lax.rem(x + z, SIDE) + 3, SIDE)
    active = here < 3
    sibling = (tm + 1 - 2 * core, sp)

    def chip(i, sign):
        dx, dz, dy = offset(i)
        cx = lax.rem(x + SIDE + sign * dx, SIDE)
        cz = lax.rem(z + SIDE + sign * dz, SIDE)
        cy = lax.rem(y + SIDE + sign * dy, SIDE)
        return cx, cz, cy

    barrier = pltpu.get_barrier_semaphore()

    def greet(i, carry):
        cx, cz, cy = chip(i, 1)
        pl.semaphore_signal(
            barrier, inc=1, device_id=(2 * cy + core, cx * SIDE + cz), device_id_type=MESH
        )
        return carry

    lax.fori_loop(1, CHIPS, greet, 0)
    pl.semaphore_signal(barrier, inc=1, device_id=sibling, device_id_type=MESH)
    pl.semaphore_wait(barrier, CHIPS)

    for d in range(1, SIDE):
        pltpu.make_async_remote_copy(
            meta_in, meta_v.at[y], m_send, m_recv,
            device_id=(2 * lax.rem(y + d, SIDE) + core, sp), device_id_type=MESH,
        ).start()
    pltpu.make_async_copy(meta_in, meta_v.at[y], m_recv).start()

    def send(src, dst, send_sem, recv_sem):
        def one(i, carry):
            cx, cz, cy = chip(i, 1)
            k = lax.rem(cy + SIDE - lax.rem(cx + cz, SIDE) + 3, SIDE)
            head = 3 * (cx * SIDE + cz) + k
            piece = src.at[:, :, pl.ds(pl.multiple_of(head * DH, DH), DH)]

            @pl.when(jnp.logical_and(k < 3, i == 0))
            def _():
                pltpu.make_async_copy(piece, dst(i), recv_sem(i)).start()

            @pl.when(jnp.logical_and(k < 3, i > 0))
            def _():
                pltpu.make_async_remote_copy(
                    piece, dst(i), send_sem, recv_sem(i),
                    device_id=(2 * cy + core, cx * SIDE + cz), device_id_type=MESH,
                ).start()

            return carry

        lax.fori_loop(0, CHIPS, one, 0)

    own = pl.ds(2 * sp, 2)
    send(k_in, lambda i: kbuf.at[own, tm], k_send, lambda i: k_recv.at[y])
    send(v_in, lambda i: vbuf.at[own, tm], v_send, lambda i: v_recv.at[y])
    send(q_in, lambda i: qbuf.at[i], q_send, lambda i: q_recv.at[i])

    pltpu.make_async_copy(meta_v, meta_v, m_recv).wait()
    move = pltpu.make_async_copy(meta_v, meta_s, m_copy)
    move.start()
    move.wait()

    @pl.when(active)
    def _():
        for buf, recv, f_send, f_recv in (
            (kbuf, k_recv, fk_send, fk_recv), (vbuf, v_recv, fv_send, fv_recv),
        ):
            for j in range(SIDE):
                half = buf.at[:, 2 * j + core]
                pltpu.make_async_copy(half, half, recv.at[j]).wait()
                pltpu.make_async_remote_copy(
                    half, half, f_send.at[j], f_recv.at[j],
                    device_id=sibling, device_id_type=MESH,
                ).start()
        for buf, f_recv in ((kbuf, fk_recv), (vbuf, fv_recv)):
            for j in range(SIDE):
                half = buf.at[:, 2 * j + 1 - core]
                pltpu.make_async_copy(half, half, f_recv.at[j]).wait()

        scale = DH ** -0.5 * math.log2(math.e)
        my_head = 3 * sp + here

        def attend(i, j, pair):
            width = 2 * (j + 1)
            keys = width * TILE
            for half in range(2):
                t = 2 * pair + half
                other = meta_s[j, 0, t]
                reach = meta_s[j, 1, t]
                q = qbuf[i, half]
                span = lax.broadcasted_iota(jnp.int32, (1, keys), 1) // TILE
                valid = jnp.logical_and(span >= reach, span <= 2 * j + core)
                bias = jnp.where(valid, 0.0, NEG)
                nt = (((1,), (1,)), ((), ()))
                k_own = kbuf[t, :width].reshape(keys, DH)
                k_other = kbuf[other, :width].reshape(keys, DH)
                s_own = lax.dot_general(q, k_own, nt, preferred_element_type=jnp.float32) + bias
                s_other = lax.dot_general(q, k_other, nt, preferred_element_type=jnp.float32) + bias
                top = jnp.max(jnp.maximum(s_own, s_other), axis=1, keepdims=True)
                e_own = jnp.exp2((s_own - top) * scale)
                e_other = jnp.exp2((s_other - top) * scale)
                total = jnp.sum(e_own + e_other, axis=1, keepdims=True)
                v_own = vbuf[t, :width].reshape(keys, DH)
                v_other = vbuf[other, :width].reshape(keys, DH)
                numer = jnp.dot(
                    e_own.astype(jnp.bfloat16), v_own, preferred_element_type=jnp.float32
                ) + jnp.dot(
                    e_other.astype(jnp.bfloat16), v_other, preferred_element_type=jnp.float32
                )
                obuf[i, half] = (numer / total).astype(jnp.bfloat16)

        def work(i, carry):
            cx, cz, cy = chip(i, -1)
            pair = cx * SIDE + cz
            pltpu.make_async_copy(qbuf.at[i], qbuf.at[i], q_recv.at[i]).wait()
            for j in range(SIDE):
                pl.when(cy == j)(functools.partial(attend, i, j, pair))
            home = out.at[:, :, pl.ds(pl.multiple_of(my_head * DH, DH), DH)]

            @pl.when(i == 0)
            def _():
                pltpu.make_async_copy(obuf.at[i], home, o_recv).start()

            @pl.when(i > 0)
            def _():
                pltpu.make_async_remote_copy(
                    obuf.at[i], home, o_send, o_recv,
                    device_id=(2 * cy + core, pair), device_id_type=MESH,
                ).start()

            return carry

        lax.fori_loop(0, CHIPS, work, 0)

        sent = obuf.at[pl.ds(1, CHIPS - 1)]
        pltpu.make_async_copy(sent, sent, o_send).wait()
        for buf, f_send in ((kbuf, fk_send), (vbuf, fv_send)):
            for j in range(SIDE):
                half = buf.at[:, 2 * j + core]
                pltpu.make_async_copy(half, half, f_send.at[j]).wait()

    for src, sem in ((q_in, q_send), (k_in, k_send), (v_in, v_send)):
        rest = src.at[:, :, pl.ds(0, (HEADS - 1) * DH)]
        pltpu.make_async_copy(rest, rest, sem).wait()

        @pl.when(jnp.logical_not(active))
        def _():
            last = src.at[:, :, pl.ds((HEADS - 1) * DH, DH)]
            pltpu.make_async_copy(last, last, sem).wait()

    lists = meta_v.at[pl.ds(0, SIDE - 1)]
    pltpu.make_async_copy(lists, lists, m_send).wait()
    pltpu.make_async_copy(out, out, o_recv).wait()


def body(queries, key_rows, value_rows, tile_lists, span_reach):
    rows, width = queries.shape
    halves = (rows // TILE, TILE, width)
    meta = jnp.concatenate([tile_lists[0, :, 1][None], span_reach], axis=0)
    meta = jnp.pad(meta, ((0, 6), (0, 128 - TILES)))
    dma = pltpu.SemaphoreType.DMA
    half_work = 2 * SPANS // 2 * TILES // 2 * 64 * 128 * 128 * 5 * 4
    out = pl.pallas_call(
        kernel,
        out_shape=jax.ShapeDtypeStruct(halves, queries.dtype),
        in_specs=[pl.BlockSpec(memory_space=pl.ANY)] * 4,
        out_specs=pl.BlockSpec(memory_space=pl.ANY),
        scratch_shapes=[
            pltpu.VMEM((CHIPS, 2, TILE, DH), jnp.bfloat16),
            pltpu.VMEM((TILES, SPANS, TILE, DH), jnp.bfloat16),
            pltpu.VMEM((TILES, SPANS, TILE, DH), jnp.bfloat16),
            pltpu.VMEM((CHIPS, 2, TILE, DH), jnp.bfloat16),
            pltpu.VMEM((SIDE, 8, 128), jnp.int32),
            pltpu.SMEM((SIDE, 8, 128), jnp.int32),
            dma, dma, dma, dma, dma,
            dma((CHIPS,)), dma((SIDE,)), dma((SIDE,)), dma, dma,
            dma((SIDE,)), dma((SIDE,)), dma((SIDE,)), dma((SIDE,)), dma,
        ],
        compiler_params=pltpu.CompilerParams(
            collective_id=0, has_side_effects=True, vmem_limit_bytes=48 << 20
        ),
        cost_estimate=pl.CostEstimate(
            flops=half_work, bytes_accessed=4 * rows * width * 2, transcendentals=half_work // 512
        ),
        name="attend",
    )(
        queries.reshape(halves), key_rows.reshape(halves), value_rows.reshape(halves), meta
    )
    return out.reshape(rows, width)


def solution(mesh):
    in_specs = (
        P(("tm", "space"), None),
        P(("tm", "space"), None),
        P(("tm", "space"), None),
        P("tm", None, None),
        P("tm", None),
    )
    return jax.shard_map(
        body, mesh=mesh, in_specs=in_specs, out_specs=P(("tm", "space"), None), check_vma=False
    )
```

time: 583 us -> 147 us (0.25)
  the two profiles are of different devices: /device:TPU:24 before, /device:TPU:9 now
where the time goes in v1:
time: 147 us
  Pallas kernels  142 us (97%)
  local copies, waits for them, and re-layouts  4.64 us (3%)
    pallas_call x1, Pallas kernels, body(): pl.pallas_call(kernel, out_shape=jax.ShapeDtypeStruct(halves, queries.dty...  142 us
    unnamed x5, local copies, waits for them, and re-layouts  3.95 us

profile of v1, /device:TPU:9, one launch (start us, length us, event | category | flops | bytes accessed | tf_op | source)
XLA Modules:
  0.0 147.0 jit_solution(16951707557082855095)
XLA Ops:
  0.0 0.7 slice_bitcast_fusion
  0.7 0.7 pad_add_fusion
  1.4 0.0 copy-start
  1.4 1.4 copy-done
  2.8 0.0 copy-start.1
  2.8 1.4 copy-done.1
  4.2 141.7 %attend.1 = bf16[2,64,6144]{2,1,0:T(8,128)(2,1)S(1)} custom-call(bf16[2,64,6144]{2,1,0:T(8,128)(2,1)S(1)} %bitcast.7, bf16[2,64,6144]{2,1,0:T(8,128)(2,1)S(1)} %bitcast.8, bf16[2,64,6144]{2,1,0:T(8,128)(2,1)} %bitcast.9, s32[8,128]{1,0:T(8,128)S(1)} %pad.4.meta_in), custom_call_target="tpu_custom_call" | custom-call | flops 2684354560 | bytes 6291456 | tf_op jit(solution)/shard_map/attend/pallas_call | solution.py:200
  145.9 1.1 copy.7
  (1 shorter events, 0.0 us)
Async XLA Ops:
  1.4 1.4 copy-start
  2.8 1.4 copy-start.1

commit v2 on v1

v2 whole, which is shorter than its diff:
```python
import math

import jax
import jax.numpy as jnp
from jax import lax
from jax.experimental import pallas as pl
from jax.experimental.pallas import tpu as pltpu
from jax.sharding import PartitionSpec as P

MESH = pl.DeviceIdType.MESH
DH = 128
TILE = 64
SIDE = 4
PLANE = SIDE * SIDE
HEADS = 48
GROUP = 3
TILES = 32
PIECES = PLANE * GROUP
NEG = -1e30
SCALE = DH ** -0.5 * math.log2(math.e)
NT = (((1,), (1,)), ((), ()))


def kernel(
    q_in, k_in, v_in, meta_in, out,
    qbuf, kbuf, vbuf, obuf, lbuf, pbuf, plog, own_o, own_l, meta_v, meta_s,
    q_send, k_send, v_send, o_send, p_send, l_send, m_send,
    q_recv, k_recv, v_recv, o_recv, p_recv, l_recv, m_recv,
    fk_send, fk_recv, fv_send, fv_recv, fq_send, m_copy,
):
    tm = lax.axis_index("tm")
    sp = lax.axis_index("space")
    y, core = tm // 2, tm % 2
    x, z = sp // SIDE, sp % SIDE
    late = y == GROUP
    early = y < GROUP
    sibling = (tm + 1 - 2 * core, sp)

    def place(i, sign):
        a, b = i % SIDE, (i // SIDE) % SIDE
        dx, dz = a, (2 * a + b) % SIDE
        return lax.rem(x + SIDE + sign * dx, SIDE) * SIDE + lax.rem(z + SIDE + sign * dz, SIDE)

    def ring(s):
        return lax.rem(y + s, GROUP)

    def wait(ref, sem):
        pltpu.make_async_copy(ref, ref, sem).wait()

    def columns(head):
        return pl.ds(pl.multiple_of(head * DH, DH), DH)

    barrier = pltpu.get_barrier_semaphore()

    def greet(i, carry):
        where = place(i, 1)
        for d in range(SIDE):
            there = 2 * lax.rem(y + d, SIDE) + core

            @pl.when(jnp.logical_or(i > 0, d > 0))
            def _():
                pl.semaphore_signal(
                    barrier, inc=1, device_id=(there, where), device_id_type=MESH
                )

        return carry

    lax.fori_loop(0, PLANE, greet, 0)
    pl.semaphore_signal(barrier, inc=1, device_id=sibling, device_id_type=MESH)
    pl.semaphore_wait(barrier, PLANE * SIDE)

    for d in range(1, SIDE):
        pltpu.make_async_remote_copy(
            meta_in, meta_v.at[y], m_send, m_recv,
            device_id=(2 * lax.rem(y + d, SIDE) + core, sp), device_id_type=MESH,
        ).start()
    pltpu.make_async_copy(meta_in, meta_v.at[y], m_recv).start()

    def send(src, dst, send_sem, recv_sem):
        def one(i, carry):
            s = lax.rem(i, GROUP)
            where = place(i, 1)
            there = jnp.where(late, GROUP, ring(s))
            head = GROUP * where + jnp.where(late, s, there)
            slot = jnp.where(late, s, y)
            piece = src.at[:, :, columns(head)]
            mine = jnp.logical_and(
                lax.rem(i, PLANE) == 0, jnp.logical_or(late, s == 0)
            )

            @pl.when(mine)
            def _():
                pltpu.make_async_copy(piece, dst(i, slot), recv_sem(i, slot)).start()

            @pl.when(jnp.logical_not(mine))
            def _():
                pltpu.make_async_remote_copy(
                    piece, dst(i, slot), send_sem, recv_sem(i, slot),
                    device_id=(2 * there + core, where), device_id_type=MESH,
                ).start()

            return carry

        lax.fori_loop(0, PIECES, one, 0)

    own = pl.ds(2 * sp, 2)
    send(k_in, lambda i, j: kbuf.at[own, 2 * j + core], k_send, lambda i, j: k_recv.at[j])
    send(v_in, lambda i, j: vbuf.at[own, 2 * j + core], v_send, lambda i, j: v_recv.at[j])
    send(q_in, lambda i, j: qbuf.at[i], q_send, lambda i, j: q_recv.at[i])

    wait(meta_v, m_recv)
    move = pltpu.make_async_copy(meta_v, meta_s, m_copy)
    move.start()
    move.wait()

    swaps = (
        (kbuf, k_recv, fk_send, fk_recv), (vbuf, v_recv, fv_send, fv_recv),
    )
    for buf, recv, f_send, f_recv in swaps:
        for j in range(GROUP):
            half = buf.at[:, 2 * j + core]
            wait(half, recv.at[j])
            pltpu.make_async_remote_copy(
                half, half, f_send.at[j], f_recv.at[j],
                device_id=sibling, device_id_type=MESH,
            ).start()
    for buf, _, _, f_recv in swaps:
        for j in range(GROUP):
            wait(buf.at[:, 2 * j + 1 - core], f_recv.at[j])

    def attend(q, t, other, first, width, valid):
        keys = width * TILE
        spans = pl.ds(first, width)
        bias = jnp.where(valid, 0.0, NEG)
        k = jnp.concatenate(
            [kbuf[t, spans].reshape(keys, DH), kbuf[other, spans].reshape(keys, DH)], axis=0
        )
        s = lax.dot_general(q, k, NT, preferred_element_type=jnp.float32)
        s = s + jnp.concatenate([bias, bias], axis=1)
        top = jnp.max(s, axis=1, keepdims=True)
        e = jnp.exp2((s - top) * SCALE).astype(jnp.bfloat16)
        v = jnp.concatenate(
            [vbuf[t, spans].reshape(keys, DH), vbuf[other, spans].reshape(keys, DH)], axis=0
        )
        v = jnp.concatenate([v, jnp.ones_like(v)], axis=1)
        r = jnp.dot(e, v, preferred_element_type=jnp.float32)
        total = r[:, DH:]
        return r[:, :DH] / total, top * SCALE + jnp.log2(total)

    def spans_of(width, first):
        return first + lax.broadcasted_iota(jnp.int32, (1, width * TILE), 1) // TILE

    def diagonal(half):
        shape = (TILE, DH)
        row = lax.broadcasted_iota(jnp.int32, shape, 0)
        lane = lax.broadcasted_iota(jnp.int32, shape, 1)
        return jnp.where(lane == row + half * TILE, 1.0, 0.0)

    @pl.when(early)
    def _():
        my_head = GROUP * sp + y
        home = out.at[:, :, columns(my_head)]

        def work(n, carry):
            items = []
            for j in range(GROUP):
                i = GROUP * n + lax.rem(y - j + GROUP, GROUP)
                items.append((i, place(i, -1)))
            items.append((PIECES + n, place(GROUP * n + y, -1)))
            for i, _ in items:
                wait(qbuf.at[i], q_recv.at[i])
            logs = []
            for j, (i, where) in enumerate(items):
                width = min(2 * (j + 1), 2 * GROUP)
                span = spans_of(width, 0)
                for half in range(2):
                    t = 2 * where + half
                    valid = span >= meta_s[j, 1, t]
                    if j < GROUP:
                        valid = jnp.logical_and(valid, span <= 2 * j + core)
                    o, log = attend(qbuf[i, half], t, meta_s[j, 0, t], 0, width, valid)
                    obuf[i, half] = o.astype(jnp.bfloat16)
                    if j == GROUP:
                        logs.append(jnp.sum(log * diagonal(half), axis=0, keepdims=True))
            lbuf[n] = jnp.broadcast_to(logs[0] + logs[1], (8, DH))
            for j, (i, where) in enumerate(items[:GROUP]):
                mine = jnp.logical_and(lax.rem(i, PLANE) == 0, j == y)

                @pl.when(mine)
                def _():
                    pltpu.make_async_copy(obuf.at[i], home, o_recv).start()

                @pl.when(jnp.logical_not(mine))
                def _():
                    pltpu.make_async_remote_copy(
                        obuf.at[i], home, o_send, o_recv,
                        device_id=(2 * j + core, where), device_id_type=MESH,
                    ).start()

            i = PIECES + n
            piece = GROUP * n + y
            above = dict(device_id=(2 * GROUP + core, sp), device_id_type=MESH)
            pltpu.make_async_remote_copy(
                obuf.at[i], pbuf.at[piece], p_send, p_recv.at[piece], **above
            ).start()
            pltpu.make_async_remote_copy(
                lbuf.at[n], plog.at[piece], l_send, l_recv.at[piece], **above
            ).start()
            return carry

        lax.fori_loop(0, PLANE, work, 0)
        wait(obuf.at[pl.ds(0, PIECES - 1)], o_send)
        wait(obuf.at[pl.ds(PIECES, PLANE)], p_send)
        wait(lbuf, l_send)

    @pl.when(late)
    def _():
        def work(n, carry):
            for h in range(GROUP):
                i = GROUP * n + h
                wait(qbuf.at[i], q_recv.at[i])
                pltpu.make_async_remote_copy(
                    qbuf.at[i], qbuf.at[PIECES + n], fq_send, q_recv.at[PIECES + n],
                    device_id=(2 * h + core, sp), device_id_type=MESH,
                ).start()
            span = spans_of(2, 2 * GROUP)
            for h in range(GROUP):
                i = GROUP * n + h
                where = place(i, -1)
                for half in range(2):
                    t = 2 * where + half
                    valid = jnp.logical_and(
                        span >= meta_s[GROUP, 1, t], span <= 2 * GROUP + core
                    )
                    o, log = attend(qbuf[i, half], t, meta_s[GROUP, 0, t], 2 * h, 2, valid)
                    own_o[i, half] = o
                    own_l[i, half] = log
            return carry

        lax.fori_loop(0, PLANE, work, 0)

        def merge(i, carry):
            wait(pbuf.at[i], p_recv.at[i])
            wait(plog.at[i], l_recv.at[i])
            where = place(i, -1)
            row = plog[i, 0:1]
            for half in range(2):
                log_b = jnp.sum(row * diagonal(half), axis=1, keepdims=True)
                log_a = own_l[i, half]
                big = jnp.maximum(log_a, log_b)
                factor_a = jnp.exp2(log_a - big)
                factor_b = jnp.exp2(log_b - big)
                numer = factor_a * own_o[i, half] + factor_b * pbuf[i, half].astype(jnp.float32)
                obuf[i, half] = (numer / (factor_a + factor_b)).astype(jnp.bfloat16)
            home = out.at[:, :, columns(GROUP * sp + lax.rem(i, GROUP))]
            mine = lax.rem(i, PLANE) == 0

            @pl.when(mine)
            def _():
                pltpu.make_async_copy(obuf.at[i], home, o_recv).start()

            @pl.when(jnp.logical_not(mine))
            def _():
                pltpu.make_async_remote_copy(
                    obuf.at[i], home, o_send, o_recv,
                    device_id=(2 * GROUP + core, where), device_id_type=MESH,
                ).start()

            return carry

        lax.fori_loop(0, PIECES, merge, 0)
        wait(obuf.at[pl.ds(0, PIECES - GROUP)], o_send)
        wait(qbuf.at[pl.ds(0, PIECES)], fq_send)

    for buf, _, f_send, _ in swaps:
        for j in range(GROUP):
            wait(buf.at[:, 2 * j + core], f_send.at[j])
    for src, sem in ((q_in, q_send), (k_in, k_send), (v_in, v_send)):
        wait(src.at[:, :, pl.ds(0, (PIECES - GROUP) * DH)], sem)

        @pl.when(early)
        def _():
            wait(src.at[:, :, pl.ds(0, (GROUP - 1) * DH)], sem)

    wait(meta_v.at[pl.ds(0, SIDE - 1)], m_send)
    wait(out, o_recv)


def body(queries, key_rows, value_rows, tile_lists, span_reach):
    rows, width = queries.shape
    halves = (rows // TILE, TILE, width)
    meta = jnp.concatenate([tile_lists[0, :, 1][None], span_reach], axis=0)
    meta = jnp.pad(meta, ((0, 6), (0, 128 - TILES)))
    dma = pltpu.SemaphoreType.DMA
    flops = 2 * 2 * 20 * TILES * TILE * 128 * DH
    out = pl.pallas_call(
        kernel,
        out_shape=jax.ShapeDtypeStruct(halves, queries.dtype),
        in_specs=[pl.BlockSpec(memory_space=pl.ANY)] * 4,
        out_specs=pl.BlockSpec(memory_space=pl.ANY),
        scratch_shapes=[
            pltpu.VMEM((PIECES + PLANE, 2, TILE, DH), jnp.bfloat16),
            pltpu.VMEM((TILES, 2 * GROUP, TILE, DH), jnp.bfloat16),
            pltpu.VMEM((TILES, 2 * GROUP, TILE, DH), jnp.bfloat16),
            pltpu.VMEM((PIECES + PLANE, 2, TILE, DH), jnp.bfloat16),
            pltpu.VMEM((PLANE, 8, DH), jnp.float32),
            pltpu.VMEM((PIECES, 2, TILE, DH), jnp.bfloat16),
            pltpu.VMEM((PIECES, 8, DH), jnp.float32),
            pltpu.VMEM((PIECES, 2, TILE, DH), jnp.float32),
            pltpu.VMEM((PIECES, 2, TILE, DH), jnp.float32),
            pltpu.VMEM((SIDE, 8, 128), jnp.int32),
            pltpu.SMEM((SIDE, 8, 128), jnp.int32),
            dma, dma, dma, dma, dma, dma, dma,
            dma((PIECES + PLANE,)), dma((GROUP,)), dma((GROUP,)), dma,
            dma((PIECES,)), dma((PIECES,)), dma,
            dma((GROUP,)), dma((GROUP,)), dma((GROUP,)), dma((GROUP,)), dma, dma,
        ],
        compiler_params=pltpu.CompilerParams(
            collective_id=0, has_side_effects=True, vmem_limit_bytes=60 << 20
        ),
        cost_estimate=pl.CostEstimate(
            flops=flops, bytes_accessed=4 * rows * width * 2, transcendentals=flops // 512
        ),
        name="attend",
    )(
        queries.reshape(halves), key_rows.reshape(halves), value_rows.reshape(halves), meta
    )
    return out.reshape(rows, width)


def solution(mesh):
    in_specs = (
        P(("tm", "space"), None),
        P(("tm", "space"), None),
        P(("tm", "space"), None),
        P("tm", None, None),
        P("tm", None),
    )
    return jax.shard_map(
        body, mesh=mesh, in_specs=in_specs, out_specs=P(("tm", "space"), None), check_vma=False
    )
```

time: 147 us -> 135 us (0.918)
  the two profiles are of different devices: /device:TPU:9 before, /device:TPU:24 now
where the time goes in v2:
time: 135 us; the launch traced here: 133 us
  Pallas kernels  128 us (95%)
  local copies, waits for them, and re-layouts  3.97 us (3%)
    pallas_call x1, Pallas kernels, body(): pl.pallas_call(kernel, out_shape=jax.ShapeDtypeStruct(halves, queries.dty...  128 us

profile of v2, /device:TPU:24, one launch (start us, length us, event | category | flops | bytes accessed | tf_op | source)
XLA Modules:
  0.0 133.0 jit_solution(4161850054450431752)
XLA Ops:
  0.0 0.7 slice_bitcast_fusion
  0.7 0.7 pad_add_fusion
  1.3 0.6 pad.4.meta_in
  1.9 128.4 %attend.1 = bf16[2,64,6144]{2,1,0:T(8,128)(2,1)} custom-call(bf16[2,64,6144]{2,1,0:T(8,128)(2,1)} %bitcast.7, bf16[2,64,6144]{2,1,0:T(8,128)(2,1)} %bitcast.8, bf16[2,64,6144]{2,1,0:T(8,128)(2,1)} %bitcast.9, s32[8,128]{1,0:T(8,128)} %pad.4.meta_in), custom_call_target="tpu_custom_call" | custom-call | flops 2684354560 | bytes 6291456 | tf_op jit(solution)/shard_map/attend/pallas_call | solution.py:296
  130.3 2.7 %copy.7 = bf16[128,6144]{1,0:T(8,128)(2,1)} copy(bf16[128,6144]{1,0:T(8,128)(2,1)} %bitcast.6) | data formatting | bytes 3145728

commit v3 on v2

--- a/solution.py
+++ b/solution.py
@@ -23,10 +23,10 @@
 
 def kernel(
     q_in, k_in, v_in, meta_in, out,
-    qbuf, kbuf, vbuf, obuf, lbuf, pbuf, plog, own_o, own_l, meta_v, meta_s,
+    qbuf, kbuf, vbuf, obuf, lbuf, pbuf, plog, own_o, own_l, kpass, vpass, meta_v, meta_s,
     q_send, k_send, v_send, o_send, p_send, l_send, m_send,
     q_recv, k_recv, v_recv, o_recv, p_recv, l_recv, m_recv,
-    fk_send, fk_recv, fv_send, fv_recv, fq_send, m_copy,
+    fk_send, fk_recv, fv_send, fv_recv, fq_send, m_copy, kp_send, kp_recv, vp_send, vp_recv,
 ):
     tm = lax.axis_index("tm")
     sp = lax.axis_index("space")
@@ -76,7 +76,7 @@
         ).start()
     pltpu.make_async_copy(meta_in, meta_v.at[y], m_recv).start()
 
-    def send(src, dst, send_sem, recv_sem):
+    def send(src, dst, send_sem, recv_sem, by_way=None):
         def one(i, carry):
             s = lax.rem(i, GROUP)
             where = place(i, 1)
@@ -92,26 +92,60 @@
             def _():
                 pltpu.make_async_copy(piece, dst(i, slot), recv_sem(i, slot)).start()
 
-            @pl.when(jnp.logical_not(mine))
+            turn = jnp.logical_and(y == 0, s == 2) if by_way else False
+
+            @pl.when(jnp.logical_not(jnp.logical_or(mine, turn)))
             def _():
                 pltpu.make_async_remote_copy(
                     piece, dst(i, slot), send_sem, recv_sem(i, slot),
                     device_id=(2 * there + core, where), device_id_type=MESH,
                 ).start()
 
+            if by_way:
+                pass_buf, pass_recv = by_way
+
+                @pl.when(turn)
+                def _():
+                    n = i // GROUP
+                    pltpu.make_async_remote_copy(
+                        piece, pass_buf.at[n], send_sem, pass_recv.at[n],
+                        device_id=(2 * GROUP + core, where // SIDE * SIDE + z),
+                        device_id_type=MESH,
+                    ).start()
+
             return carry
 
         lax.fori_loop(0, PIECES, one, 0)
 
     own = pl.ds(2 * sp, 2)
-    send(k_in, lambda i, j: kbuf.at[own, 2 * j + core], k_send, lambda i, j: k_recv.at[j])
-    send(v_in, lambda i, j: vbuf.at[own, 2 * j + core], v_send, lambda i, j: v_recv.at[j])
+    send(k_in, lambda i, j: kbuf.at[own, 2 * j + core], k_send, lambda i, j: k_recv.at[j], (kpass, kp_recv))
+    send(v_in, lambda i, j: vbuf.at[own, 2 * j + core], v_send, lambda i, j: v_recv.at[j], (vpass, vp_recv))
     send(q_in, lambda i, j: qbuf.at[i], q_send, lambda i, j: q_recv.at[i])
 
     wait(meta_v, m_recv)
     move = pltpu.make_async_copy(meta_v, meta_s, m_copy)
     move.start()
     move.wait()
+
+    passes = (
+        (kpass, kp_send, kp_recv, kbuf, k_recv), (vpass, vp_send, vp_recv, vbuf, v_recv),
+    )
+
+    @pl.when(late)
+    def _():
+        for pass_buf, pass_send, pass_recv, buf, recv in passes:
+            def onward(n, carry):
+                i = GROUP * n + 2
+                wait(pass_buf.at[n], pass_recv.at[n])
+                source = place(i, -1) // SIDE * SIDE + z
+                target = x * SIDE + place(i, 1) % SIDE
+                pltpu.make_async_remote_copy(
+                    pass_buf.at[n], buf.at[pl.ds(2 * source, 2), core], pass_send, recv.at[0],
+                    device_id=(2 * 2 + core, target), device_id_type=MESH,
+                ).start()
+                return carry
+
+            lax.fori_loop(0, PLANE, onward, 0)
 
     swaps = (
         (kbuf, k_recv, fk_send, fk_recv), (vbuf, v_recv, fv_send, fv_recv),
@@ -128,24 +162,33 @@
         for j in range(GROUP):
             wait(buf.at[:, 2 * j + 1 - core], f_recv.at[j])
 
-    def attend(q, t, other, first, width, valid):
-        keys = width * TILE
-        spans = pl.ds(first, width)
-        bias = jnp.where(valid, 0.0, NEG)
-        k = jnp.concatenate(
-            [kbuf[t, spans].reshape(keys, DH), kbuf[other, spans].reshape(keys, DH)], axis=0
-        )
-        s = lax.dot_general(q, k, NT, preferred_element_type=jnp.float32)
-        s = s + jnp.concatenate([bias, bias], axis=1)
-        top = jnp.max(s, axis=1, keepdims=True)
-        e = jnp.exp2((s - top) * SCALE).astype(jnp.bfloat16)
-        v = jnp.concatenate(
-            [vbuf[t, spans].reshape(keys, DH), vbuf[other, spans].reshape(keys, DH)], axis=0
-        )
-        v = jnp.concatenate([v, jnp.ones_like(v)], axis=1)
-        r = jnp.dot(e, v, preferred_element_type=jnp.float32)
-        total = r[:, DH:]
-        return r[:, :DH] / total, top * SCALE + jnp.log2(total)
+    def attend(tasks):
+        def rows(buf, t, other, first, width):
+            spans, keys = pl.ds(first, width), width * TILE
+            return jnp.concatenate(
+                [buf[t, spans].reshape(keys, DH), buf[other, spans].reshape(keys, DH)], axis=0
+            )
+
+        scores = []
+        for q, t, other, first, width, valid in tasks:
+            bias = jnp.where(valid, 0.0, NEG)
+            s = lax.dot_general(
+                q, rows(kbuf, t, other, first, width), NT, preferred_element_type=jnp.float32
+            )
+            scores.append(s + jnp.concatenate([bias, bias], axis=1))
+        tops = [jnp.max(s, axis=1, keepdims=True) for s in scores]
+        weights = [
+            jnp.exp2((s - top) * SCALE).astype(jnp.bfloat16) for s, top in zip(scores, tops)
+        ]
+        sums = []
+        for e, (_, t, other, first, width, _) in zip(weights, tasks):
+            v = rows(vbuf, t, other, first, width)
+            v = jnp.concatenate([v, jnp.ones_like(v)], axis=1)
+            sums.append(jnp.dot(e, v, preferred_element_type=jnp.float32))
+        return [
+            (r[:, :DH] / r[:, DH:], lambda r=r, top=top: top * SCALE + jnp.log2(r[:, DH:]))
+            for r, top in zip(sums, tops)
+        ]
 
     def spans_of(width, first):
         return first + lax.broadcasted_iota(jnp.int32, (1, width * TILE), 1) // TILE
@@ -169,7 +212,7 @@
             items.append((PIECES + n, place(GROUP * n + y, -1)))
             for i, _ in items:
                 wait(qbuf.at[i], q_recv.at[i])
-            logs = []
+            tasks = []
             for j, (i, where) in enumerate(items):
                 width = min(2 * (j + 1), 2 * GROUP)
                 span = spans_of(width, 0)
@@ -178,10 +221,13 @@
                     valid = span >= meta_s[j, 1, t]
                     if j < GROUP:
                         valid = jnp.logical_and(valid, span <= 2 * j + core)
-                    o, log = attend(qbuf[i, half], t, meta_s[j, 0, t], 0, width, valid)
-                    obuf[i, half] = o.astype(jnp.bfloat16)
-                    if j == GROUP:
-                        logs.append(jnp.sum(log * diagonal(half), axis=0, keepdims=True))
+                    tasks.append((qbuf[i, half], t, meta_s[j, 0, t], 0, width, valid))
+            logs = []
+            for task, (o, log) in enumerate(attend(tasks)):
+                j, half = task // 2, task % 2
+                obuf[items[j][0], half] = o.astype(jnp.bfloat16)
+                if j == GROUP:
+                    logs.append(jnp.sum(log() * diagonal(half), axis=0, keepdims=True))
             lbuf[n] = jnp.broadcast_to(logs[0] + logs[1], (8, DH))
             for j, (i, where) in enumerate(items[:GROUP]):
                 mine = jnp.logical_and(lax.rem(i, PLANE) == 0, j == y)
@@ -224,6 +270,7 @@
                     device_id=(2 * h + core, sp), device_id_type=MESH,
                 ).start()
             span = spans_of(2, 2 * GROUP)
+            tasks = []
             for h in range(GROUP):
                 i = GROUP * n + h
                 where = place(i, -1)
@@ -232,9 +279,11 @@
                     valid = jnp.logical_and(
                         span >= meta_s[GROUP, 1, t], span <= 2 * GROUP + core
                     )
-                    o, log = attend(qbuf[i, half], t, meta_s[GROUP, 0, t], 2 * h, 2, valid)
-                    own_o[i, half] = o
-                    own_l[i, half] = log
+                    tasks.append((qbuf[i, half], t, meta_s[GROUP, 0, t], 2 * h, 2, valid))
+            for task, (o, log) in enumerate(attend(tasks)):
+                i, half = GROUP * n + task // 2, task % 2
+                own_o[i, half] = o
+                own_l[i, half] = log()
             return carry
 
         lax.fori_loop(0, PLANE, work, 0)
@@ -271,6 +320,8 @@
         lax.fori_loop(0, PIECES, merge, 0)
         wait(obuf.at[pl.ds(0, PIECES - GROUP)], o_send)
         wait(qbuf.at[pl.ds(0, PIECES)], fq_send)
+        for pass_buf, pass_send, _, _, _ in passes:
+            wait(pass_buf, pass_send)
 
     for buf, _, f_send, _ in swaps:
         for j in range(GROUP):
@@ -296,7 +347,7 @@
     out = pl.pallas_call(
         kernel,
         out_shape=jax.ShapeDtypeStruct(halves, queries.dtype),
-        in_specs=[pl.BlockSpec(memory_space=pl.ANY)] * 4,
+        in_specs=[pl.BlockSpec(memory_space=pltpu.HBM)] * 3 + [pl.BlockSpec(memory_space=pl.ANY)],
         out_specs=pl.BlockSpec(memory_space=pl.ANY),
         scratch_shapes=[
             pltpu.VMEM((PIECES + PLANE, 2, TILE, DH), jnp.bfloat16),
@@ -308,12 +359,15 @@
             pltpu.VMEM((PIECES, 8, DH), jnp.float32),
             pltpu.VMEM((PIECES, 2, TILE, DH), jnp.float32),
             pltpu.VMEM((PIECES, 2, TILE, DH), jnp.float32),
+            pltpu.VMEM((PLANE, 2, TILE, DH), jnp.bfloat16),
+            pltpu.VMEM((PLANE, 2, TILE, DH), jnp.bfloat16),
             pltpu.VMEM((SIDE, 8, 128), jnp.int32),
             pltpu.SMEM((SIDE, 8, 128), jnp.int32),
             dma, dma, dma, dma, dma, dma, dma,
             dma((PIECES + PLANE,)), dma((GROUP,)), dma((GROUP,)), dma,
             dma((PIECES,)), dma((PIECES,)), dma,
             dma((GROUP,)), dma((GROUP,)), dma((GROUP,)), dma((GROUP,)), dma, dma,
+            dma, dma((PLANE,)), dma, dma((PLANE,)),
         ],
         compiler_params=pltpu.CompilerParams(
             collective_id=0, has_side_effects=True, vmem_limit_bytes=60 << 20

time: 135 us -> 100 us (0.74)
  Pallas kernels: 128 us -> 94.2 us
    pallas_call x1, Pallas kernels: 128 us -> 94.2 us  [body(): pl.pallas_call(kernel, out_shape=jax.ShapeDtypeStruct(halves, queries.dty...]
where the time goes in v3:
time: 100 us; the launch traced here: 98.8 us
  Pallas kernels  94.2 us (94%)
  local copies, waits for them, and re-layouts  3.97 us (4%)
    pallas_call x1, Pallas kernels, body(): pl.pallas_call(kernel, out_shape=jax.ShapeDtypeStruct(halves, queries.dty...  94.2 us
    unnamed x1, local copies, waits for them, and re-layouts  2.69 us

profile of v3, /device:TPU:24, one launch (start us, length us, event | category | flops | bytes accessed | tf_op | source)
XLA Modules:
  0.0 98.8 jit_solution(9263571651808449137)
XLA Ops:
  0.0 0.7 slice_bitcast_fusion
  0.7 0.7 pad_add_fusion
  1.3 0.6 pad.4.meta_in
  1.9 94.2 %attend.1 = bf16[2,64,6144]{2,1,0:T(8,128)(2,1)} custom-call(bf16[2,64,6144]{2,1,0:T(8,128)(2,1)} %bitcast.7, bf16[2,64,6144]{2,1,0:T(8,128)(2,1)} %bitcast.8, bf16[2,64,6144]{2,1,0:T(8,128)(2,1)} %bitcast.9, s32[8,128]{1,0:T(8,128)} %pad.4.meta_in), custom_call_target="tpu_custom_call" | custom-call | flops 2684354560 | bytes 6291456 | tf_op jit(solution)/shard_map/attend/pallas_call | solution.py:347
  96.1 2.7 %copy.7 = bf16[128,6144]{1,0:T(8,128)(2,1)} copy(bf16[128,6144]{1,0:T(8,128)(2,1)} %bitcast.6) | data formatting | bytes 3145728

commit v4 on v3

v4 whole, which is shorter than its diff:
```python
import math

import jax
import jax.numpy as jnp
from jax import lax
from jax.experimental import pallas as pl
from jax.experimental.pallas import tpu as pltpu
from jax.sharding import PartitionSpec as P

MESH = pl.DeviceIdType.MESH
DH = 128
TILE = 64
SIDE = 4
PLANE = SIDE * SIDE
HEADS = 48
GROUP = 3
TILES = 32
PIECES = PLANE * GROUP
BATCH = 4
NEG = -1e30
SCALE = DH ** -0.5 * math.log2(math.e)
NT = (((1,), (1,)), ((), ()))


def kernel(
    q_in, k_in, v_in, lists_in, reach_in, out,
    qbuf, kbuf, vbuf, obuf, lbuf, pbuf, plog, vpass, qpass, lists_v, reach_v, lists_s, reach_s,
    q_send, k_send, v_send, o_send, p_send, l_send, m_send,
    q_recv, k_recv, v_recv, o_recv, p_recv, l_recv, m_recv,
    fk_send, fk_recv, fv_send, fv_recv, fq_send, m_copy, vp_send, vp_recv, qp_send, qp_recv,
):
    tm = lax.axis_index("tm")
    sp = lax.axis_index("space")
    y, core = tm // 2, tm % 2
    x, z = sp // SIDE, sp % SIDE
    late = y == GROUP
    early = y < GROUP
    sibling = (tm + 1 - 2 * core, sp)

    def place(i, sign):
        a, b = i % SIDE, (i // SIDE) % SIDE
        dx, dz = a, (2 * a + b) % SIDE
        return lax.rem(x + SIDE + sign * dx, SIDE) * SIDE + lax.rem(z + SIDE + sign * dz, SIDE)

    def ring(s):
        return lax.rem(y + s, GROUP)

    def wait(ref, sem):
        pltpu.make_async_copy(ref, ref, sem).wait()

    def columns(head):
        return pl.ds(pl.multiple_of(head * DH, DH), DH)

    barrier = pltpu.get_barrier_semaphore()

    def greet(i, carry):
        where = place(i, 1)
        for d in range(SIDE):
            there = 2 * lax.rem(y + d, SIDE) + core

            @pl.when(jnp.logical_or(i > 0, d > 0))
            def _():
                pl.semaphore_signal(
                    barrier, inc=1, device_id=(there, where), device_id_type=MESH
                )

        return carry

    lax.fori_loop(0, PLANE, greet, 0)
    pl.semaphore_signal(barrier, inc=1, device_id=sibling, device_id_type=MESH)
    pl.semaphore_wait(barrier, PLANE * SIDE)

    lists = ((lists_in, lists_v, lists_s), (reach_in, reach_v, reach_s))
    for k, (src, dst, _) in enumerate(lists):
        for d in range(1, SIDE):
            pltpu.make_async_remote_copy(
                src, dst.at[y], m_send.at[k], m_recv.at[k],
                device_id=(2 * lax.rem(y + d, SIDE) + core, sp), device_id_type=MESH,
            ).start()
        pltpu.make_async_copy(src, dst.at[y], m_recv.at[k]).start()

    def send(kind, src, dst, send_sem, recv_sem, by_way=None):
        def one(i, carry):
            s = lax.rem(i, GROUP)
            where = place(i, 1)
            there = GROUP if kind == "late" else ring(s)
            head = GROUP * where + (s if kind == "late" else there)
            piece = src.at[:, :, columns(head)]
            mine = lax.rem(i, PLANE) == 0
            if kind == "early":
                mine = jnp.logical_and(mine, s == 0)
            turn = jnp.logical_and(y == 0, s == 2) if by_way else False

            @pl.when(mine)
            def _():
                pltpu.make_async_copy(piece, dst(i), recv_sem.at[i]).start()

            @pl.when(jnp.logical_not(jnp.logical_or(mine, turn)))
            def _():
                pltpu.make_async_remote_copy(
                    piece, dst(i), send_sem, recv_sem.at[i],
                    device_id=(2 * there + core, where), device_id_type=MESH,
                ).start()

            if by_way:
                pass_buf, pass_recv = by_way

                @pl.when(turn)
                def _():
                    n = i // GROUP
                    pltpu.make_async_remote_copy(
                        piece, pass_buf.at[n], send_sem, pass_recv.at[n],
                        device_id=(2 * GROUP + core, where // SIDE * SIDE + z),
                        device_id_type=MESH,
                    ).start()

            return carry

        lax.fori_loop(0, PIECES, one, 0)

    def span_slot(buf, pair, j):
        return buf.at[pl.ds(2 * pair, 2), 2 * j + core]

    def swap(i, j, buf, recv, f_send, f_recv):
        piece = span_slot(buf, place(i, -1), j)
        wait(piece, recv.at[i])
        pltpu.make_async_remote_copy(
            piece, piece, f_send, f_recv, device_id=sibling, device_id_type=MESH
        ).start()

    def onward(n, pass_buf, pass_send, pass_recv, dst, recv):
        i = GROUP * n + 2
        wait(pass_buf.at[n], pass_recv.at[n])
        pltpu.make_async_remote_copy(
            pass_buf.at[n], dst(i), pass_send, recv.at[i],
            device_id=(2 * 2 + core, x * SIDE + place(i, 1) % SIDE), device_id_type=MESH,
        ).start()

    def from_zero(buf):
        return lambda i: span_slot(buf, place(i, -1) // SIDE * SIDE + z, 0)

    swap_k = (kbuf, k_recv, fk_send, fk_recv)
    swap_v = (vbuf, v_recv, fv_send, fv_recv)
    pass_v = (vpass, vp_send, vp_recv, from_zero(vbuf), v_recv)
    pass_q = (qpass, qp_send, qp_recv, lambda i: qbuf.at[i], q_recv)

    def lists_ready():
        for k, (_, buf, _) in enumerate(lists):
            wait(buf, m_recv.at[k])
        moves = [pltpu.make_async_copy(v, s, m_copy.at[k]) for k, (_, v, s) in enumerate(lists)]
        for move in moves:
            move.start()
        for move in moves:
            move.wait()

    def swapped():
        wait(kbuf.at[:, pl.ds(0, GROUP)], fk_recv)
        wait(vbuf.at[:, pl.ds(0, GROUP)], fv_recv)

    @pl.when(early)
    def _():
        send("early", k_in, lambda i: span_slot(kbuf, sp, y), k_send, k_recv)
        send("early", v_in, lambda i: span_slot(vbuf, sp, y), v_send, v_recv, (vpass, vp_recv))
        send("early", q_in, lambda i: qbuf.at[i], q_send, q_recv, (qpass, qp_recv))
        lists_ready()
        for what in (swap_k, swap_v):
            def pieces(i, carry):
                swap(i, lax.rem(y + GROUP - lax.rem(i, GROUP), GROUP), *what)
                return carry

            lax.fori_loop(0, PIECES, pieces, 0)
        swapped()

    @pl.when(late)
    def _():
        send("late", q_in, lambda i: qbuf.at[i], q_send, q_recv)
        send("late", k_in, lambda i: span_slot(kbuf, sp, lax.rem(i, GROUP)), k_send, k_recv)
        send("late", v_in, lambda i: span_slot(vbuf, sp, lax.rem(i, GROUP)), v_send, v_recv)
        lists_ready()

        def first(n, carry):
            for h in range(GROUP):
                i = GROUP * n + h
                wait(qbuf.at[i], q_recv.at[i])
                pltpu.make_async_remote_copy(
                    qbuf.at[i], qbuf.at[PIECES + n], fq_send, q_recv.at[PIECES + n],
                    device_id=(2 * h + core, sp), device_id_type=MESH,
                ).start()
            return carry

        lax.fori_loop(0, PLANE, first, 0)

        def second(n, carry):
            onward(n, *pass_v)
            return carry

        lax.fori_loop(0, PLANE, second, 0)

        def third(i, carry):
            swap(i, lax.rem(i, GROUP), *swap_k)
            return carry

        lax.fori_loop(0, PIECES, third, 0)

        def fourth(n, carry):
            for h in range(GROUP):
                swap(GROUP * n + h, h, *swap_v)
            onward(n, *pass_q)
            return carry

        lax.fori_loop(0, PLANE, fourth, 0)
        swapped()

    def attend(tasks):
        def rows(buf, t, other, first, width):
            spans, keys = pl.ds(first, width), width * TILE
            return jnp.concatenate(
                [buf[t, spans].reshape(keys, DH), buf[other, spans].reshape(keys, DH)], axis=0
            )

        scores = []
        for q, t, other, first, width, valid in tasks:
            bias = jnp.where(valid, 0.0, NEG)
            s = lax.dot_general(
                q, rows(kbuf, t, other, first, width), NT, preferred_element_type=jnp.float32
            )
            scores.append(s + jnp.concatenate([bias, bias], axis=1))
        tops = [jnp.max(s, axis=1, keepdims=True) for s in scores]
        weights = [
            jnp.exp2((s - top) * SCALE).astype(jnp.bfloat16) for s, top in zip(scores, tops)
        ]
        sums = []
        for e, (_, t, other, first, width, _) in zip(weights, tasks):
            v = rows(vbuf, t, other, first, width)
            v = jnp.concatenate([v, jnp.ones_like(v)], axis=1)
            sums.append(jnp.dot(e, v, preferred_element_type=jnp.float32))
        return [
            (r[:, :DH] / r[:, DH:], lambda r=r, top=top: top * SCALE + jnp.log2(r[:, DH:]))
            for r, top in zip(sums, tops)
        ]

    def spans_of(width, first):
        return first + lax.broadcasted_iota(jnp.int32, (1, width * TILE), 1) // TILE

    def diagonal(half):
        shape = (TILE, DH)
        row = lax.broadcasted_iota(jnp.int32, shape, 0)
        lane = lax.broadcasted_iota(jnp.int32, shape, 1)
        return jnp.where(lane == row + half * TILE, 1.0, 0.0)

    @pl.when(early)
    def _():
        home = out.at[:, :, columns(GROUP * sp + y)]

        def task(i, half, j, pair):
            width = min(2 * (j + 1), 2 * GROUP)
            span = spans_of(width, 0)
            t = 2 * pair + half
            valid = span >= reach_s[j, 0, t]
            if j < GROUP:
                valid = jnp.logical_and(valid, span <= 2 * j + core)
            return qbuf[i, half], t, lists_s[j, 1, t], 0, width, valid

        def last_spans(m, carry):
            chunks = [BATCH * m + c for c in range(BATCH)]
            for n in chunks:
                wait(qbuf.at[PIECES + n], q_recv.at[PIECES + n])
            done = attend([
                task(PIECES + n, half, GROUP, place(GROUP * n + y, -1))
                for n in chunks for half in range(2)
            ])
            for c, n in enumerate(chunks):
                log = 0.0
                for half in range(2):
                    o, logs = done[2 * c + half]
                    obuf[PIECES + n, half] = o.astype(jnp.bfloat16)
                    log = log + jnp.sum(logs() * diagonal(half), axis=0, keepdims=True)
                lbuf[n] = jnp.broadcast_to(log, (8, DH))
            for n in chunks:
                piece = GROUP * n + y
                above = dict(device_id=(2 * GROUP + core, sp), device_id_type=MESH)
                pltpu.make_async_remote_copy(
                    obuf.at[PIECES + n], pbuf.at[piece], p_send, p_recv.at[piece], **above
                ).start()
                pltpu.make_async_remote_copy(
                    lbuf.at[n], plog.at[piece], l_send, l_recv.at[piece], **above
                ).start()
            return carry

        lax.fori_loop(0, PLANE // BATCH, last_spans, 0)

        def work(n, carry):
            items = []
            for j in range(GROUP):
                i = GROUP * n + lax.rem(y - j + GROUP, GROUP)
                items.append((i, place(i, -1)))
            for i, _ in items:
                wait(qbuf.at[i], q_recv.at[i])
            done = attend([
                task(i, half, j, pair)
                for j, (i, pair) in enumerate(items) for half in range(2)
            ])
            for j, (i, pair) in enumerate(items):
                for half in range(2):
                    obuf[i, half] = done[2 * j + half][0].astype(jnp.bfloat16)
                mine = jnp.logical_and(lax.rem(i, PLANE) == 0, j == y)

                @pl.when(mine)
                def _():
                    pltpu.make_async_copy(obuf.at[i], home, o_recv).start()

                @pl.when(jnp.logical_not(mine))
                def _():
                    pltpu.make_async_remote_copy(
                        obuf.at[i], home, o_send, o_recv,
                        device_id=(2 * j + core, pair), device_id_type=MESH,
                    ).start()

            return carry

        lax.fori_loop(0, PLANE, work, 0)
        wait(obuf.at[pl.ds(0, PIECES - 1)], o_send)
        wait(obuf.at[pl.ds(PIECES, PLANE)], p_send)
        wait(lbuf, l_send)

    @pl.when(late)
    def _():
        def work(n, carry):
            pieces = [GROUP * n + h for h in range(GROUP)]
            span = spans_of(2, 2 * GROUP)
            tasks = []
            for h, i in enumerate(pieces):
                pair = place(i, -1)
                for half in range(2):
                    t = 2 * pair + half
                    valid = jnp.logical_and(
                        span >= reach_s[GROUP, 0, t], span <= 2 * GROUP + core
                    )
                    tasks.append((qbuf[i, half], t, lists_s[GROUP, 1, t], 2 * h, 2, valid))
            done = attend(tasks)
            for i in pieces:
                wait(pbuf.at[i], p_recv.at[i])
                wait(plog.at[i], l_recv.at[i])
            merged = []
            for k, (o, log) in enumerate(done):
                i, half = pieces[k // 2], k % 2
                log_a = log()
                log_b = jnp.sum(plog[i, 0:1] * diagonal(half), axis=1, keepdims=True)
                big = jnp.maximum(log_a, log_b)
                factor_a = jnp.exp2(log_a - big)
                factor_b = jnp.exp2(log_b - big)
                numer = factor_a * o + factor_b * pbuf[i, half].astype(jnp.float32)
                merged.append((numer / (factor_a + factor_b)).astype(jnp.bfloat16))
            for k, o in enumerate(merged):
                obuf[pieces[k // 2], k % 2] = o
            for h, i in enumerate(pieces):
                home = out.at[:, :, columns(GROUP * sp + h)]
                mine = lax.rem(i, PLANE) == 0

                @pl.when(mine)
                def _():
                    pltpu.make_async_copy(obuf.at[i], home, o_recv).start()

                @pl.when(jnp.logical_not(mine))
                def _():
                    pltpu.make_async_remote_copy(
                        obuf.at[i], home, o_send, o_recv,
                        device_id=(2 * GROUP + core, place(i, -1)), device_id_type=MESH,
                    ).start()

            return carry

        lax.fori_loop(0, PLANE, work, 0)
        wait(obuf.at[pl.ds(0, PIECES - GROUP)], o_send)
        wait(qbuf.at[pl.ds(0, PIECES)], fq_send)
        wait(vpass, vp_send)
        wait(qpass, qp_send)

    wait(kbuf.at[:, pl.ds(0, GROUP)], fk_send)
    wait(vbuf.at[:, pl.ds(0, GROUP)], fv_send)
    for src, sem in ((q_in, q_send), (k_in, k_send), (v_in, v_send)):
        wait(src.at[:, :, pl.ds(0, (PIECES - GROUP) * DH)], sem)

        @pl.when(early)
        def _():
            wait(src.at[:, :, pl.ds(0, (GROUP - 1) * DH)], sem)

    for k, (_, buf, _) in enumerate(lists):
        wait(buf.at[pl.ds(0, SIDE - 1)], m_send.at[k])
    wait(out, o_recv)


def body(queries, key_rows, value_rows, tile_lists, span_reach):
    rows, width = queries.shape
    halves = (rows // TILE, TILE, width)
    dma = pltpu.SemaphoreType.DMA
    flops = 2 * 2 * 20 * TILES * TILE * 128 * DH
    out = pl.pallas_call(
        kernel,
        out_shape=jax.ShapeDtypeStruct(halves, queries.dtype),
        in_specs=[pl.BlockSpec(memory_space=pltpu.HBM)] * 3 + [pl.BlockSpec(memory_space=pl.ANY)] * 2,
        out_specs=pl.BlockSpec(memory_space=pl.ANY),
        scratch_shapes=[
            pltpu.VMEM((PIECES + PLANE, 2, TILE, DH), jnp.bfloat16),
            pltpu.VMEM((TILES, 2 * GROUP, TILE, DH), jnp.bfloat16),
            pltpu.VMEM((TILES, 2 * GROUP, TILE, DH), jnp.bfloat16),
            pltpu.VMEM((PIECES + PLANE, 2, TILE, DH), jnp.bfloat16),
            pltpu.VMEM((PLANE, 8, DH), jnp.float32),
            pltpu.VMEM((PIECES, 2, TILE, DH), jnp.bfloat16),
            pltpu.VMEM((PIECES, 8, DH), jnp.float32),
            pltpu.VMEM((PLANE, 2, TILE, DH), jnp.bfloat16),
            pltpu.VMEM((PLANE, 2, TILE, DH), jnp.bfloat16),
            pltpu.VMEM((SIDE, 2, TILES), jnp.int32),
            pltpu.VMEM((SIDE, 1, TILES), jnp.int32),
            pltpu.SMEM((SIDE, 2, TILES), jnp.int32),
            pltpu.SMEM((SIDE, 1, TILES), jnp.int32),
            dma, dma, dma, dma, dma, dma, dma((2,)),
            dma((PIECES + PLANE,)), dma((PIECES,)), dma((PIECES,)), dma,
            dma((PIECES,)), dma((PIECES,)), dma((2,)),
            dma, dma, dma, dma, dma, dma((2,)),
            dma, dma((PLANE,)), dma, dma((PLANE,)),
        ],
        compiler_params=pltpu.CompilerParams(
            collective_id=0, has_side_effects=True, vmem_limit_bytes=48 << 20
        ),
        cost_estimate=pl.CostEstimate(
            flops=flops, bytes_accessed=4 * rows * width * 2, transcendentals=flops // 512
        ),
        name="attend",
    )(
        *(
            pltpu.with_memory_space_constraint(array, pltpu.HBM)
            for array in (
                queries.reshape(halves), key_rows.reshape(halves), value_rows.reshape(halves),
                tile_lists[0].T, span_reach,
            )
        ),
    )
    return out.reshape(rows, width)


def solution(mesh):
    in_specs = (
        P(("tm", "space"), None),
        P(("tm", "space"), None),
        P(("tm", "space"), None),
        P("tm", None, None),
        P("tm", None),
    )
    return jax.shard_map(
        body, mesh=mesh, in_specs=in_specs, out_specs=P(("tm", "space"), None), check_vma=False
    )
```

time: 100 us -> 94.6 us (0.946)
  local copies, waits for them, and re-layouts: 3.97 us -> 1.15 us
  Pallas kernels: 94.2 us -> 92.1 us
    pallas_call x1, Pallas kernels: 94.2 us -> 92.1 us  [body(): pl.pallas_call(kernel, out_shape=jax.ShapeDtypeStruct(halves, queries.dty...]
    unnamed x1, local copies, waits for them, and re-layouts: 2.69 us -> 1.15 us
where the time goes in v4:
time: 94.6 us; the launch traced here: 93.3 us
  Pallas kernels  92.1 us (97%)
  local copies, waits for them, and re-layouts  1.15 us (1%)
    pallas_call x1, Pallas kernels, body(): pl.pallas_call(kernel, out_shape=jax.ShapeDtypeStruct(halves, queries.dty...  92.1 us

profile of v4, /device:TPU:24, one launch (start us, length us, event | category | flops | bytes accessed | tf_op | source)
XLA Modules:
  0.0 93.3 jit_solution(9649844733631926692)
XLA Ops:
  0.0 92.1 %attend.1 = bf16[2,64,6144]{2,1,0:T(8,128)(2,1)S(1)} custom-call(bf16[2,64,6144]{2,1,0:T(8,128)(2,1)} %bitcast.8, bf16[2,64,6144]{2,1,0:T(8,128)(2,1)} %bitcast.9, bf16[2,64,6144]{2,1,0:T(8,128)(2,1)} %bitcast.10, s32[2,32]{1,0:T(2,128)} %bitcast.11, s32[1,32]{1,0:T(1,128)} %reach_in.1), custom_call_target="tpu_custom_call" | custom-call | flops 2684354560 | bytes 6291456 | tf_op jit(solution)/shard_map/attend/pallas_call | solution.py:398
  92.1 1.1 %copy.7 = bf16[128,6144]{1,0:T(8,128)(2,1)} copy(bf16[128,6144]{1,0:T(8,128)(2,1)S(1)} %bitcast.7) | data formatting | bytes 3145728

commit v5 on v4

--- a/solution.py
+++ b/solution.py
@@ -16,7 +16,8 @@
 GROUP = 3
 TILES = 32
 PIECES = PLANE * GROUP
-BATCH = 4
+BATCH = 2
+STEP = 2
 NEG = -1e30
 SCALE = DH ** -0.5 * math.log2(math.e)
 NT = (((1,), (1,)), ((), ()))
@@ -53,20 +54,15 @@
 
     barrier = pltpu.get_barrier_semaphore()
 
-    def greet(i, carry):
-        where = place(i, 1)
-        for d in range(SIDE):
-            there = 2 * lax.rem(y + d, SIDE) + core
-
-            @pl.when(jnp.logical_or(i > 0, d > 0))
-            def _():
-                pl.semaphore_signal(
-                    barrier, inc=1, device_id=(there, where), device_id_type=MESH
-                )
-
-        return carry
-
-    lax.fori_loop(0, PLANE, greet, 0)
+    for dx in range(SIDE):
+        for dz in range(SIDE):
+            for dy in range(SIDE):
+                if dx or dz or dy:
+                    where = lax.rem(x + dx, SIDE) * SIDE + lax.rem(z + dz, SIDE)
+                    pl.semaphore_signal(
+                        barrier, inc=1, device_id=(2 * lax.rem(y + dy, SIDE) + core, where),
+                        device_id_type=MESH,
+                    )
     pl.semaphore_signal(barrier, inc=1, device_id=sibling, device_id_type=MESH)
     pl.semaphore_wait(barrier, PLANE * SIDE)
 
@@ -226,17 +222,15 @@
             )
             scores.append(s + jnp.concatenate([bias, bias], axis=1))
         tops = [jnp.max(s, axis=1, keepdims=True) for s in scores]
-        weights = [
-            jnp.exp2((s - top) * SCALE).astype(jnp.bfloat16) for s, top in zip(scores, tops)
-        ]
+        weights = [jnp.exp2((s - top) * SCALE) for s, top in zip(scores, tops)]
+        totals = [jnp.sum(e, axis=1, keepdims=True) for e in weights]
         sums = []
         for e, (_, t, other, first, width, _) in zip(weights, tasks):
             v = rows(vbuf, t, other, first, width)
-            v = jnp.concatenate([v, jnp.ones_like(v)], axis=1)
-            sums.append(jnp.dot(e, v, preferred_element_type=jnp.float32))
+            sums.append(jnp.dot(e.astype(jnp.bfloat16), v, preferred_element_type=jnp.float32))
         return [
-            (r[:, :DH] / r[:, DH:], lambda r=r, top=top: top * SCALE + jnp.log2(r[:, DH:]))
-            for r, top in zip(sums, tops)
+            (r / total, lambda top=top, total=total: top * SCALE + jnp.log2(total))
+            for r, top, total in zip(sums, tops, totals)
         ]
 
     def spans_of(width, first):
@@ -287,22 +281,20 @@
                 ).start()
             return carry
 
-        lax.fori_loop(0, PLANE // BATCH, last_spans, 0)
-
-        def work(n, carry):
+        def work(m, carry):
             items = []
-            for j in range(GROUP):
-                i = GROUP * n + lax.rem(y - j + GROUP, GROUP)
-                items.append((i, place(i, -1)))
-            for i, _ in items:
+            for n in [STEP * m + c for c in range(STEP)]:
+                for j in range(GROUP):
+                    i = GROUP * n + lax.rem(y - j + GROUP, GROUP)
+                    items.append((i, j, place(i, -1)))
+            for i, _, _ in items:
                 wait(qbuf.at[i], q_recv.at[i])
             done = attend([
-                task(i, half, j, pair)
-                for j, (i, pair) in enumerate(items) for half in range(2)
+                task(i, half, j, pair) for i, j, pair in items for half in range(2)
             ])
-            for j, (i, pair) in enumerate(items):
+            for k, (i, j, pair) in enumerate(items):
                 for half in range(2):
-                    obuf[i, half] = done[2 * j + half][0].astype(jnp.bfloat16)
+                    obuf[i, half] = done[2 * k + half][0].astype(jnp.bfloat16)
                 mine = jnp.logical_and(lax.rem(i, PLANE) == 0, j == y)
 
                 @pl.when(mine)
@@ -318,7 +310,14 @@
 
             return carry
 
-        lax.fori_loop(0, PLANE, work, 0)
+        def both(m, carry):
+            last_spans(m + 1, 0)
+            work(m, 0)
+            return carry
+
+        lax.fori_loop(0, 1, last_spans, 0)
+        lax.fori_loop(0, PLANE // BATCH - 1, both, 0)
+        lax.fori_loop(PLANE // BATCH - 1, PLANE // STEP, work, 0)
         wait(obuf.at[pl.ds(0, PIECES - 1)], o_send)
         wait(obuf.at[pl.ds(PIECES, PLANE)], p_send)
         wait(lbuf, l_send)

time: 94.6 us -> 93.7 us (level)
  no operation moved by 1% of the time
where the time goes in v5:
time: 93.7 us; the launch traced here: 92.5 us
  Pallas kernels  91.3 us (97%)
  local copies, waits for them, and re-layouts  1.15 us (1%)
    pallas_call x1, Pallas kernels, body(): pl.pallas_call(kernel, out_shape=jax.ShapeDtypeStruct(halves, queries.dty...  91.3 us

profile of v5, /device:TPU:24, one launch (start us, length us, event | category | flops | bytes accessed | tf_op | source)
XLA Modules:
  0.0 92.5 jit_solution(11512300768696755353)
XLA Ops:
  0.0 91.3 %attend.1 = bf16[2,64,6144]{2,1,0:T(8,128)(2,1)S(1)} custom-call(bf16[2,64,6144]{2,1,0:T(8,128)(2,1)} %bitcast.8, bf16[2,64,6144]{2,1,0:T(8,128)(2,1)} %bitcast.9, bf16[2,64,6144]{2,1,0:T(8,128)(2,1)} %bitcast.10, s32[2,32]{1,0:T(2,128)} %bitcast.11, s32[1,32]{1,0:T(1,128)} %reach_in.1), custom_call_target="tpu_custom_call" | custom-call | flops 2684354560 | bytes 6291456 | tf_op jit(solution)/shard_map/attend/pallas_call | solution.py:397
  91.3 1.1 %copy.7 = bf16[128,6144]{1,0:T(8,128)(2,1)} copy(bf16[128,6144]{1,0:T(8,128)(2,1)S(1)} %bitcast.7) | data formatting | bytes 3145728

commit v6 on v5

--- a/solution.py
+++ b/solution.py
@@ -40,7 +40,7 @@
 
     def place(i, sign):
         a, b = i % SIDE, (i // SIDE) % SIDE
-        dx, dz = a, (2 * a + b) % SIDE
+        dx, dz = (2 * a + 3 * b) % SIDE, (3 * a) % SIDE
         return lax.rem(x + SIDE + sign * dx, SIDE) * SIDE + lax.rem(z + SIDE + sign * dz, SIDE)
 
     def ring(s):

time: 93.7 us -> 92.4 us (0.986); the launches traced: 92.5 us -> 92.3 us
  no operation moved by 1% of the time
where the time goes in v6:
time: 92.4 us; the launch traced here: 92.3 us
  Pallas kernels  91.2 us (99%)
  local copies, waits for them, and re-layouts  1.15 us (1%)
    pallas_call x1, Pallas kernels, body(): pl.pallas_call(kernel, out_shape=jax.ShapeDtypeStruct(halves, queries.dty...  91.2 us

profile of v6, /device:TPU:24, one launch (start us, length us, event | category | flops | bytes accessed | tf_op | source)
XLA Modules:
  0.0 92.3 jit_solution(14748996305712776582)
XLA Ops:
  0.0 91.2 %attend.1 = bf16[2,64,6144]{2,1,0:T(8,128)(2,1)S(1)} custom-call(bf16[2,64,6144]{2,1,0:T(8,128)(2,1)} %bitcast.8, bf16[2,64,6144]{2,1,0:T(8,128)(2,1)} %bitcast.9, bf16[2,64,6144]{2,1,0:T(8,128)(2,1)} %bitcast.10, s32[2,32]{1,0:T(2,128)} %bitcast.11, s32[1,32]{1,0:T(1,128)} %reach_in.1), custom_call_target="tpu_custom_call" | custom-call | flops 2684354560 | bytes 6291456 | tf_op jit(solution)/shard_map/attend/pallas_call | solution.py:397
  91.2 1.1 %copy.7 = bf16[128,6144]{1,0:T(8,128)(2,1)} copy(bf16[128,6144]{1,0:T(8,128)(2,1)S(1)} %bitcast.7) | data formatting | bytes 3145728

commit v7 on v6

--- a/solution.py
+++ b/solution.py
@@ -25,10 +25,10 @@
 
 def kernel(
     q_in, k_in, v_in, lists_in, reach_in, out,
-    qbuf, kbuf, vbuf, obuf, lbuf, pbuf, plog, vpass, qpass, lists_v, reach_v, lists_s, reach_s,
+    qbuf, kbuf, vbuf, obuf, lbuf, pbuf, plog, kpass, qpass, lists_v, reach_v, lists_s, reach_s,
     q_send, k_send, v_send, o_send, p_send, l_send, m_send,
     q_recv, k_recv, v_recv, o_recv, p_recv, l_recv, m_recv,
-    fk_send, fk_recv, fv_send, fv_recv, fq_send, m_copy, vp_send, vp_recv, qp_send, qp_recv,
+    fk_send, fk_recv, fv_send, fv_recv, fq_send, m_copy, kp_send, kp_recv, qp_send, qp_recv,
 ):
     tm = lax.axis_index("tm")
     sp = lax.axis_index("space")
@@ -40,7 +40,7 @@
 
     def place(i, sign):
         a, b = i % SIDE, (i // SIDE) % SIDE
-        dx, dz = (2 * a + 3 * b) % SIDE, (3 * a) % SIDE
+        dx, dz = (3 * b + 2 * a) % SIDE, (3 * a + 2 * b) % SIDE
         return lax.rem(x + SIDE + sign * dx, SIDE) * SIDE + lax.rem(z + SIDE + sign * dz, SIDE)
 
     def ring(s):
@@ -137,7 +137,7 @@
 
     swap_k = (kbuf, k_recv, fk_send, fk_recv)
     swap_v = (vbuf, v_recv, fv_send, fv_recv)
-    pass_v = (vpass, vp_send, vp_recv, from_zero(vbuf), v_recv)
+    pass_k = (kpass, kp_send, kp_recv, from_zero(kbuf), k_recv)
     pass_q = (qpass, qp_send, qp_recv, lambda i: qbuf.at[i], q_recv)
 
     def lists_ready():
@@ -155,8 +155,8 @@
 
     @pl.when(early)
     def _():
-        send("early", k_in, lambda i: span_slot(kbuf, sp, y), k_send, k_recv)
-        send("early", v_in, lambda i: span_slot(vbuf, sp, y), v_send, v_recv, (vpass, vp_recv))
+        send("early", k_in, lambda i: span_slot(kbuf, sp, y), k_send, k_recv, (kpass, kp_recv))
+        send("early", v_in, lambda i: span_slot(vbuf, sp, y), v_send, v_recv)
         send("early", q_in, lambda i: qbuf.at[i], q_send, q_recv, (qpass, qp_recv))
         lists_ready()
         for what in (swap_k, swap_v):
@@ -175,6 +175,7 @@
         lists_ready()
 
         def first(n, carry):
+            onward(n, *pass_k)
             for h in range(GROUP):
                 i = GROUP * n + h
                 wait(qbuf.at[i], q_recv.at[i])
@@ -186,12 +187,6 @@
 
         lax.fori_loop(0, PLANE, first, 0)
 
-        def second(n, carry):
-            onward(n, *pass_v)
-            return carry
-
-        lax.fori_loop(0, PLANE, second, 0)
-
         def third(i, carry):
             swap(i, lax.rem(i, GROUP), *swap_k)
             return carry
@@ -199,12 +194,16 @@
         lax.fori_loop(0, PIECES, third, 0)
 
         def fourth(n, carry):
-            for h in range(GROUP):
-                swap(GROUP * n + h, h, *swap_v)
             onward(n, *pass_q)
             return carry
 
         lax.fori_loop(0, PLANE, fourth, 0)
+
+        def fifth(i, carry):
+            swap(i, lax.rem(i, GROUP), *swap_v)
+            return carry
+
+        lax.fori_loop(0, PIECES, fifth, 0)
         swapped()
 
     def attend(tasks):
@@ -372,7 +371,7 @@
         lax.fori_loop(0, PLANE, work, 0)
         wait(obuf.at[pl.ds(0, PIECES - GROUP)], o_send)
         wait(qbuf.at[pl.ds(0, PIECES)], fq_send)
-        wait(vpass, vp_send)
+        wait(kpass, kp_send)
         wait(qpass, qp_send)
 
     wait(kbuf.at[:, pl.ds(0, GROUP)], fk_send)

time: 92.4 us -> 91.7 us (level)
  no operation moved by 1% of the time
where the time goes in v7:
time: 91.7 us; the launch traced here: 91.6 us
  Pallas kernels  90.5 us (99%)
  local copies, waits for them, and re-layouts  1.15 us (1%)
    pallas_call x1, Pallas kernels, body(): pl.pallas_call(kernel, out_shape=jax.ShapeDtypeStruct(halves, queries.dty...  90.5 us

profile of v7, /device:TPU:24, one launch (start us, length us, event | category | flops | bytes accessed | tf_op | source)
XLA Modules:
  0.0 91.6 jit_solution(16315507605994667351)
XLA Ops:
  0.0 90.5 %attend.1 = bf16[2,64,6144]{2,1,0:T(8,128)(2,1)S(1)} custom-call(bf16[2,64,6144]{2,1,0:T(8,128)(2,1)} %bitcast.8, bf16[2,64,6144]{2,1,0:T(8,128)(2,1)} %bitcast.9, bf16[2,64,6144]{2,1,0:T(8,128)(2,1)} %bitcast.10, s32[2,32]{1,0:T(2,128)} %bitcast.11, s32[1,32]{1,0:T(1,128)} %reach_in.1), custom_call_target="tpu_custom_call" | custom-call | flops 2684354560 | bytes 6291456 | tf_op jit(solution)/shard_map/attend/pallas_call | solution.py:396
  90.5 1.1 %copy.7 = bf16[128,6144]{1,0:T(8,128)(2,1)} copy(bf16[128,6144]{1,0:T(8,128)(2,1)S(1)} %bitcast.7) | data formatting | bytes 3145728

commit v8 on v7

--- a/solution.py
+++ b/solution.py
@@ -67,13 +67,15 @@
     pl.semaphore_wait(barrier, PLANE * SIDE)
 
     lists = ((lists_in, lists_v, lists_s), (reach_in, reach_v, reach_s))
-    for k, (src, dst, _) in enumerate(lists):
-        for d in range(1, SIDE):
-            pltpu.make_async_remote_copy(
-                src, dst.at[y], m_send.at[k], m_recv.at[k],
-                device_id=(2 * lax.rem(y + d, SIDE) + core, sp), device_id_type=MESH,
-            ).start()
-        pltpu.make_async_copy(src, dst.at[y], m_recv.at[k]).start()
+
+    def send_lists():
+        for k, (src, dst, _) in enumerate(lists):
+            for d in range(1, SIDE):
+                pltpu.make_async_remote_copy(
+                    src, dst.at[y], m_send.at[k], m_recv.at[k],
+                    device_id=(2 * lax.rem(y + d, SIDE) + core, sp), device_id_type=MESH,
+                ).start()
+            pltpu.make_async_copy(src, dst.at[y], m_recv.at[k]).start()
 
     def send(kind, src, dst, send_sem, recv_sem, by_way=None):
         def one(i, carry):
@@ -156,6 +158,7 @@
     @pl.when(early)
     def _():
         send("early", k_in, lambda i: span_slot(kbuf, sp, y), k_send, k_recv, (kpass, kp_recv))
+        send_lists()
         send("early", v_in, lambda i: span_slot(vbuf, sp, y), v_send, v_recv)
         send("early", q_in, lambda i: qbuf.at[i], q_send, q_recv, (qpass, qp_recv))
         lists_ready()
@@ -171,6 +174,7 @@
     def _():
         send("late", q_in, lambda i: qbuf.at[i], q_send, q_recv)
         send("late", k_in, lambda i: span_slot(kbuf, sp, lax.rem(i, GROUP)), k_send, k_recv)
+        send_lists()
         send("late", v_in, lambda i: span_slot(vbuf, sp, lax.rem(i, GROUP)), v_send, v_recv)
         lists_ready()
 

time: 91.7 us -> 93.9 us (1.024)
  Pallas kernels: 90.5 us -> 91.8 us
    pallas_call x1, Pallas kernels: 90.5 us -> 91.8 us  [body(): pl.pallas_call(kernel, out_shape=jax.ShapeDtypeStruct(halves, queries.dty...]
where the time goes in v8:
time: 93.9 us; the launch traced here: 93 us
  Pallas kernels  91.8 us (98%)
  local copies, waits for them, and re-layouts  1.15 us (1%)
    pallas_call x1, Pallas kernels, body(): pl.pallas_call(kernel, out_shape=jax.ShapeDtypeStruct(halves, queries.dty...  91.8 us

profile of v8, /device:TPU:24, one launch (start us, length us, event | category | flops | bytes accessed | tf_op | source)
XLA Modules:
  0.0 93.0 jit_solution(8967077110039859798)
XLA Ops:
  0.0 91.8 %attend.1 = bf16[2,64,6144]{2,1,0:T(8,128)(2,1)S(1)} custom-call(bf16[2,64,6144]{2,1,0:T(8,128)(2,1)} %bitcast.8, bf16[2,64,6144]{2,1,0:T(8,128)(2,1)} %bitcast.9, bf16[2,64,6144]{2,1,0:T(8,128)(2,1)} %bitcast.10, s32[2,32]{1,0:T(2,128)} %bitcast.11, s32[1,32]{1,0:T(1,128)} %reach_in.1), custom_call_target="tpu_custom_call" | custom-call | flops 2684354560 | bytes 6291456 | tf_op jit(solution)/shard_map/attend/pallas_call | solution.py:400
  91.8 1.1 %copy.7 = bf16[128,6144]{1,0:T(8,128)(2,1)} copy(bf16[128,6144]{1,0:T(8,128)(2,1)S(1)} %bitcast.7) | data formatting | bytes 3145728
